TPU v7x, 512 devices: a whole 4x8x8 slice. The times are simulated.
512 devices in a mesh: row: 16 (over y, x_hi), col: 8 (over z), depth: 4 (over x_lo, core).
Axes of the slice: x: 4 (x_hi: 2, x_lo: 2; x = x_hi * 2 + x_lo), y: 8, z: 8, core: 2. Of those that a mesh axis runs over, the one named last changes fastest.
Arguments:
- slab_parts: float32 [4, 32768, 2048], P('depth', 'row', 'col'), may hold values from -6 to 6
- panel_t: float32 [256, 32768], P('col', 'row'), may hold values from -6 to 6
- l_inv: float32 [256, 256], replicated, as said below
- u_inv: float32 [256, 256], replicated, as said below
- pivots: int32 [256], replicated, may hold values from 0 to 32767, as said below
Outputs:
- updated: float32 [32768, 2048], P(('row', 'depth'), 'col')
Inputs may be any that keep to these rules, and one draw needn't show every extreme that they name: `pivots`: entry i lies between i and 32767; entry 0 is 0. `l_inv`: unit lower triangular. `u_inv`: upper triangular with a positive diagonal.
All inputs are finite; a program needn't handle non-finite values.
Results may differ from a plain program's by a relative error of at most 0.00007.
Values sent between devices are 32-bit elements; how exact they have to be, the bound alone decides.
No kernel may reach another device: no remote copies, remote signals or barrier semaphores. Data moves between devices by JAX's collectives and lax.ppermute only.
A program may use at most 64 MiB of HBM per device.

v0:
```python
import jax
import jax.numpy as jnp
from jax import lax
from jax.sharding import PartitionSpec as P


def touched_sources(pivots, targets):
    panel_width = pivots.shape[0]
    same = targets[:, None] == targets[None, :]
    first_slot = jnp.argmax(same, axis=1)

    def swap_one(i, values):
        slot_a = first_slot[i]
        slot_b = first_slot[panel_width + i]
        value_a = values[slot_a]
        value_b = values[slot_b]
        return values.at[slot_a].set(value_b).at[slot_b].set(value_a)

    values = lax.fori_loop(0, panel_width, swap_one, targets, unroll=8)
    return values[first_slot]


def shards(slab_parts, panel_t, l_inv, u_inv, pivots):
    highest = lax.Precision.HIGHEST
    slab_local = slab_parts[0]
    row_count = slab_local.shape[0]
    panel_width = l_inv.shape[0]
    row_start = lax.axis_index("row") * row_count
    layer_index = lax.axis_index("depth")
    first_layer = layer_index == 0
    targets = jnp.concatenate([jnp.arange(panel_width, dtype=jnp.int32), pivots])
    sources = touched_sources(pivots, targets)
    owned_rows = (sources >= row_start) & (sources < row_start + row_count)
    local_index = jnp.clip(sources - row_start, 0, row_count - 1)
    slab_send = jnp.where(owned_rows[:, None], slab_local[local_index], 0.0)
    panel_owned = owned_rows & first_layer
    panel_send = jnp.where(panel_owned[None, :], panel_t[:, local_index], 0.0)
    moved_slab, moved_panel = lax.psum((slab_send, panel_send), ("row", "depth"))
    dest_index = targets - row_start
    dest_index = jnp.where((dest_index >= 0) & (dest_index < row_count), dest_index, row_count)
    layer_moved = jnp.where(first_layer, moved_slab, 0.0)
    slab_p = slab_local.at[dest_index].set(layer_moved, mode="drop")
    panel_p = panel_t.at[:, dest_index].set(moved_panel, mode="drop")
    quarter = panel_width // lax.axis_size("depth")
    q_start = layer_index * quarter
    u_cols = lax.dynamic_slice_in_dim(u_inv, q_start, quarter, 1)
    l_rows = lax.dynamic_slice_in_dim(l_inv, q_start, quarter, 0)
    contract_first = (((0,), (0,)), ((), ()))
    lower_t = lax.dot_general(
        u_cols,
        lax.all_gather(panel_p, "col", axis=0, tiled=True),
        contract_first,
        precision=highest,
        preferred_element_type=jnp.float32,
    )
    upper_rows = jnp.dot(
        l_rows, moved_slab[:panel_width], precision=highest, preferred_element_type=jnp.float32
    )
    update = slab_p - lax.dot_general(
        lower_t, upper_rows, contract_first, precision=highest, preferred_element_type=jnp.float32
    )
    global_row = row_start + jnp.arange(row_count, dtype=jnp.int32)
    top_mask = global_row < panel_width
    offset = global_row - q_start
    in_quarter = (offset >= 0) & (offset < quarter)
    top_value = jnp.where(in_quarter[:, None], upper_rows[jnp.clip(offset, 0, quarter - 1)], 0.0)
    partial_sum = jnp.where(top_mask[:, None], top_value, update)
    share_rows = row_count // lax.axis_size("depth")
    d_start = layer_index * share_rows
    summed = lax.dynamic_slice_in_dim(lax.psum(partial_sum, "depth"), d_start, share_rows, 0)
    return summed


def solution(mesh):
    placed = (P("depth", "row", "col"), P("col", "row"), P(), P(), P())
    return jax.shard_map(
        shards, mesh=mesh, in_specs=placed, out_specs=P(("row", "depth"), "col"), check_vma=False
    )
```

profile of v0, /device:TPU:1, one launch (start us, length us, event | category | flops | bytes accessed | tf_op | source)
XLA Modules:
  0.0 1904.0 jit_solution(521728760786289125)
XLA Ops:
  6.5 1.6 copy.44
  8.2 1.1 iota_reduce_fusion
  9.3 1552.5 %while.35 = (s32[]{:T(128)}, s32[512]{0:T(512)S(1)}, s32[512]{0:T(512)S(1)}, s32[]{:T(128)}, s32[]{:T(128)}, /*index=5*/s32[]{:T(128)}, s32[]{:T(128)}, s32[]{:T...) while((s32[]{:T(128)}, s32[512]{0:T(512)S(1)}, ...), condition=%wide.region_2.0_spmd.clone.clone, body=%wide.region_1.2_spmd.clone.clone.clone.sunk | while | flops 178 | bytes 18789 | solution.py:19
  86.8 0.9 select_dynamic-update-slice_fusion.40
  135.3 0.9 select_dynamic-update-slice_fusion.40
  183.9 0.9 select_dynamic-update-slice_fusion.40
  232.4 0.9 select_dynamic-update-slice_fusion.40
  329.4 0.9 select_dynamic-update-slice_fusion.40
  426.5 0.9 select_dynamic-update-slice_fusion.40
  475.0 0.9 select_dynamic-update-slice_fusion.40
  523.5 0.9 select_dynamic-update-slice_fusion.40
  572.0 0.9 select_dynamic-update-slice_fusion.40
  669.0 0.9 select_dynamic-update-slice_fusion.40
  717.6 0.9 select_dynamic-update-slice_fusion.40
  766.1 0.9 select_dynamic-update-slice_fusion.40
  1561.8 3.5 gather_fusion
  1565.4 1.3 copy.14
  1566.6 2.2 gather_fusion.1
  1568.9 1.6 gather_fusion.3
  1570.5 2.0 broadcast_select_fusion
  1572.5 1.8 select_bitcast_fusion
  1574.4 198.6 %all-reduce.6.cloned.1.call-done = (f32[512,256]{1,0:T(8,128)}, f32[32,512]{0,1:T(8,128)}) async-done(((f32[512,256]{1,0:T(8,128)}, f32[32,512]{0,1:T(8,128)}), (f32[512,256]{1,0:T(8,128)}, f32[32,512]{0,1:T(8,128)})) %all-reduce.6.cloned.1.call-update) | async-done | bytes 589840 | tf_op jit(solution)/shard_map/psum | solution.py:38
  1773.0 2.5 scatter_custom_fusion.1
  1775.5 1.0 copy.15
  1776.7 3.2 scatter_custom_fusion
  1780.0 1.1 fusion.3
  1781.1 8.6 gather_fusion.2
  1789.6 28.5 %all-gather.2.cloned.1.call-done = f32[256,2048]{1,0:T(8,128)} async-done(((f32[32,2048]{1,0:T(8,128)}), f32[256,2048]{1,0:T(8,128)}) %all-gather.2.cloned.1.call-update) | async-done | bytes 2097168 | tf_op jit(solution)/shard_map/all_gather | solution.py:51
  1818.1 3.2 fusion.9
  1821.3 3.5 fusion
  1824.9 70.7 %all-reduce.4.cloned.1.call-done = f32[2048,256]{1,0:T(8,128)} async-done(((f32[2048,256]{1,0:T(8,128)}), f32[2048,256]{1,0:T(8,128)}) %all-reduce.4.cloned.1.call-update) | async-done | bytes 2097168 | tf_op jit(solution)/shard_map/psum | solution.py:70
  1895.6 1.9 constant_dynamic-slice_fusion
  (815 shorter events, 583.6 us)
Async XLA Ops:
  6.5 1811.6 %copy-start = (f32[256,256]{1,0:T(8,128)S(1)}, f32[256,256]{1,0:T(8,128)}, u32[]{:S(2)}) copy-start(f32[256,256]{1,0:T(8,128)} %param.42) | copy-start | bytes 786436
  6.5 1.7 copy-start.3
  6.5 1766.5 %all-reduce.6.cloned.1.call-start = ((), (), s32[]{:S(2)}) async-start(), calls=%async_computation.2 | async-start | bytes 1572864 | tf_op jit(solution)/shard_map/psum | solution.py:38
  1574.3 243.8 %all-gather.2.cloned.1.call-start = ((), (), s32[]{:S(2)}) async-start(), calls=%async_computation | async-start | bytes 2359296 | tf_op jit(solution)/shard_map/all_gather | solution.py:51
  1776.6 3.4 copy-start.2
  1776.6 119.0 %all-reduce.4.cloned.1.call-start = ((), (), s32[]{:S(2)}) async-start(), calls=%async_computation.1 | async-start | bytes 4194304 | tf_op jit(solution)/shard_map/psum | solution.py:70
  1818.1 3.2 copy-start.1
Sparse Core Ops, SparseCore 0:
  1574.4 198.5 all-reduce.5
  1776.7 41.3 all-gather.1
  1825.0 70.5 all-reduce.3
where the time goes:
time: 1920 us; the launch traced here: 1900 us
  loops' own time  959 us (50%)
  other arithmetic  419 us (22%)
  waiting for transfers between devices  298 us (16%)
  local copies, waits for them, and re-layouts  207 us (11%)
    another operation x1, loops' own time, touched_sources(): values = lax.fori_loop(0, panel_width, swap_one, targets, unroll=8)  959 us
    scatter x512, other arithmetic, swap_one(): return values.at[slot_a].set(value_b).at[slot_b].set(value_a)  411 us
    psum x1, waiting for transfers between devices, shards(): lax.psum((slab_send, panel_send), ('row', 'depth'))  199 us
    another operation x256, local copies, waits for them, and re-layouts  160 us
    psum x1, waiting for transfers between devices, shards(): lax.psum(partial_sum, 'depth')  70.7 us
  transfers between devices with their start and end apart: 3, of which 3 were waited for; matrix products, arithmetic and copies ran while one was open for 1% of the time, Pallas kernels for 0%

commit v1 on v0

v1 whole, which is shorter than its diff:
```python
import functools

import jax
import jax.numpy as jnp
from jax import lax
from jax.experimental import pallas as pl
from jax.experimental.pallas import tpu as pltpu
from jax.sharding import Mesh
from jax.sharding import PartitionSpec as P

ROW = ("y", "xh")
DEPTH = ("xl", "core")
PLANE = ("xh", "xl", "core")
HIGHEST = lax.Precision.HIGHEST
F32 = jnp.float32
I32 = jnp.int32
VMEM = pl.BlockSpec(memory_space=pltpu.VMEM)
SMEM = pl.BlockSpec(memory_space=pltpu.SMEM)
ANY = pl.BlockSpec(memory_space=pl.ANY)


def lane_lookup(table, index):
    width = table.shape[1]
    parts = []
    for at in range(0, width, 128):
        wanted = index[:, at : at + 128]
        found = jnp.zeros_like(wanted)
        for start in range(0, width, 128):
            chunk = table[:, start : start + 128]
            taken = jnp.take_along_axis(chunk, wanted & 127, axis=1)
            found = jnp.where((wanted >= start) & (wanted < start + 128), taken, found)
        parts.append(found)
    return jnp.concatenate(parts, axis=1)


def pivot_kernel(place, pivots, slab_hbm, send, top_row, top_col, slab, source_v, source_s, sems):
    rows, columns = slab.shape
    width = pivots.shape[1]
    groups, both, _ = send.shape
    block = both // 2
    share = top_row.shape[1]
    row_start = place[0]
    share_start = place[1]
    fetch = pltpu.make_async_copy(slab_hbm, slab, sems.at[0])
    fetch.start()
    along = lax.broadcasted_iota(I32, (width, width), 1)
    down = lax.broadcasted_iota(I32, (width, width), 0)
    pivot_row = pivots[...]
    pivot_all = jnp.broadcast_to(pivot_row, (width, width))
    pivot_col = jnp.max(jnp.where(along == down, pivot_all, -1), axis=1, keepdims=True)
    earlier = down < along
    same = pivot_col == pivot_all
    before = jnp.max(jnp.where((pivot_col == along) & earlier, down, -1), axis=0, keepdims=True)
    last = jnp.max(jnp.where(same & earlier, down, -1), axis=0, keepdims=True)
    later = jnp.max(jnp.where(same & (down > along), 1, 0), axis=0, keepdims=True)
    slots = lax.broadcasted_iota(I32, (8, width), 1)
    before = jnp.broadcast_to(before, (8, width))
    content = jnp.where(before < 0, slots, before)
    span = 1
    while span < width:
        content = lane_lookup(content, content)
        span *= 2
    last = jnp.broadcast_to(last, (8, width))
    source = jnp.where(
        last < 0,
        jnp.broadcast_to(pivot_row, (8, width)),
        lane_lookup(content, jnp.maximum(last, 0)),
    )
    source_v[...] = source
    to_scalar = pltpu.make_async_copy(source_v, source_s, sems.at[1])
    to_scalar.start()
    content_row = content[:1]
    target_row = jnp.where((later == 0) & (pivot_row >= width), pivot_row, -1)
    content_col = jnp.max(
        jnp.where(along == down, jnp.broadcast_to(content_row, (width, width)), -1),
        axis=1,
        keepdims=True,
    )
    target_col = jnp.max(
        jnp.where(along == down, jnp.broadcast_to(target_row, (width, width)), -1),
        axis=1,
        keepdims=True,
    )
    own_along = share_start + lax.broadcasted_iota(I32, (width, share), 1)
    top_row[...] = jnp.max(jnp.where(target_col == own_along, content_col, -1), axis=0, keepdims=True)
    own_down = share_start + lax.broadcasted_iota(I32, (share, width), 0)
    found = jnp.max(jnp.where(target_row == own_down, content_row, -1), axis=1, keepdims=True)
    top_col[...] = jnp.broadcast_to(found, top_col.shape)
    fetch.wait()
    for group in range(groups):
        send[group, block:, :] = slab[group * block : (group + 1) * block, :]
    to_scalar.wait()

    def gather(group, carry):
        for slot in range(block):
            local = source_s[0, group * block + slot] - row_start
            owned = (local >= 0) & (local < rows)
            at = jnp.where(owned, local, 0)
            keep = jnp.where(owned, 1.0, 0.0).astype(F32)
            send[group, slot : slot + 1, :] = slab[pl.ds(at, 1), :] * keep
        return carry

    lax.fori_loop(0, groups, gather, 0)


def plane_sum_kernel(got, send):
    groups, both, _ = got.shape
    block = both // 2
    first = groups // 2
    moved = got[0, :block, :]
    for source in range(1, groups):
        moved = moved + got[source, :block, :]
    top = got[0, block:, :]
    for source in range(1, first):
        top = top + got[source, block:, :]
    for target in range(send.shape[0]):
        send[target, :block, :] = moved
        send[target, block:, :] = top


def column_kernel(place, got, panel, top_panel, top_row, rows_out, panel_out):
    groups, both, _ = got.shape
    block = both // 2
    moved = got[0, :block, :]
    for source in range(1, groups):
        moved = moved + got[source, :block, :]
    rows_out[:block, :] = moved
    rows_out[block:, :] = got[0, block:, :]
    share = top_row.shape[1]
    width = top_panel.shape[1]
    lands = top_row[...]
    slot = lax.broadcasted_iota(I32, (width, share), 0)
    chosen = jnp.where(slot == lands, 1.0, 0.0).astype(F32)
    replaced = jnp.dot(top_panel[...], chosen, precision=HIGHEST, preferred_element_type=F32)
    own = panel[:, pl.ds(pl.multiple_of(place[2] * share, share), share)]
    fixed = jnp.where(lands >= 0, replaced, own)
    for target in range(panel_out.shape[0]):
        panel_out[target] = fixed


def update_kernel(place, slab, panel, rows_in, l_inv, u_inv, top_col, out):
    groups, both, columns = rows_in.shape
    block = both // 2
    width = l_inv.shape[0]
    share = slab.shape[0]
    panel_p = panel[...].reshape(width, share)
    lower = lax.dot_general(
        panel_p, u_inv[...], (((0,), (0,)), ((), ())), precision=HIGHEST, preferred_element_type=F32
    )
    moved = rows_in[:, :block, :].reshape(width, columns)
    top = rows_in[:, block:, :].reshape(width, columns)
    upper = jnp.dot(l_inv[...], moved, precision=HIGHEST, preferred_element_type=F32)
    lands = top_col[:, :1]
    slot = lax.broadcasted_iota(I32, (share, width), 1)
    chosen = jnp.where(slot == lands, 1.0, 0.0).astype(F32)
    replaced = jnp.dot(chosen, top, precision=HIGHEST, preferred_element_type=F32)
    slab_p = jnp.where(lands >= 0, replaced, slab[...])
    out[...] = slab_p - jnp.dot(lower, upper, precision=HIGHEST, preferred_element_type=F32)

    @pl.when(place[1] == 0)
    def _():
        out[:width, :] = upper


def shards(slab_parts, panel_t, l_inv, u_inv, pivots):
    slab_local = slab_parts[0]
    rows, columns = slab_local.shape
    width = l_inv.shape[0]
    tall = panel_t.shape[0]
    n_y, n_z = lax.axis_size("y"), lax.axis_size("z")
    n_depth = lax.axis_size(DEPTH)
    n_plane = lax.axis_size(PLANE)
    share = rows // n_depth
    block = width // n_plane
    row_index = lax.axis_index(ROW)
    layer = lax.axis_index(DEPTH)
    row_start = row_index * rows
    place = jnp.stack([row_start, row_start + layer * share, layer]).astype(I32)

    slab_sum = lax.psum_scatter(slab_local, DEPTH, scatter_dimension=0, tiled=True)

    send, top_row, top_col = pl.pallas_call(
        pivot_kernel,
        out_shape=(
            jax.ShapeDtypeStruct((n_plane, 2 * block, columns), F32),
            jax.ShapeDtypeStruct((1, share), I32),
            jax.ShapeDtypeStruct((share, 128), I32),
        ),
        in_specs=[SMEM, VMEM, ANY],
        out_specs=(VMEM, VMEM, VMEM),
        scratch_shapes=[
            pltpu.VMEM((rows, columns), F32),
            pltpu.VMEM((8, width), I32),
            pltpu.SMEM((8, width), I32),
            pltpu.SemaphoreType.DMA((2,)),
        ],
        compiler_params=pltpu.CompilerParams(vmem_limit_bytes=32 << 20),
        name="pivot_rows",
    )(place, pivots.reshape(1, width), slab_local)

    top_panel = jnp.where(row_index == 0, panel_t[:, :width], 0.0)
    step = n_y // 2
    while step >= 1:
        pairs = [(at, at + step) for at in range(0, n_y, 2 * step)]
        top_panel = top_panel + lax.ppermute(top_panel, "y", pairs)
        step //= 2
    top_panel = top_panel + lax.ppermute(top_panel, "xh", [(0, 1)])

    got = lax.all_to_all(send, PLANE, 0, 0)
    send = pl.pallas_call(
        plane_sum_kernel,
        out_shape=jax.ShapeDtypeStruct((n_y, 2 * block, columns), F32),
        in_specs=[VMEM],
        out_specs=VMEM,
        compiler_params=pltpu.CompilerParams(vmem_limit_bytes=32 << 20),
        name="plane_sum",
    )(got)
    got = lax.all_to_all(send, "y", 0, 0)
    rows_out, panel_out = pl.pallas_call(
        column_kernel,
        out_shape=(
            jax.ShapeDtypeStruct((2 * block, columns), F32),
            jax.ShapeDtypeStruct((n_z, tall, share), F32),
        ),
        in_specs=[SMEM, VMEM, VMEM, VMEM, VMEM],
        out_specs=(VMEM, VMEM),
        compiler_params=pltpu.CompilerParams(vmem_limit_bytes=32 << 20),
        name="column_sum",
    )(place, got, panel_t, top_panel, top_row)
    panel_p = lax.all_to_all(panel_out, "z", 0, 0)
    rows_in = lax.all_gather(rows_out, PLANE)
    return pl.pallas_call(
        update_kernel,
        out_shape=jax.ShapeDtypeStruct((share, columns), F32),
        in_specs=[SMEM, VMEM, VMEM, VMEM, VMEM, VMEM, VMEM],
        out_specs=VMEM,
        compiler_params=pltpu.CompilerParams(vmem_limit_bytes=32 << 20),
        name="update_rows",
    )(place, slab_sum, panel_p, rows_in, l_inv, u_inv, top_col)


def solution(mesh):
    n_row, n_col, n_depth = mesh.devices.shape
    fine = Mesh(
        mesh.devices.reshape(n_row // 2, 2, n_col, n_depth // 2, 2), ("y", "xh", "z", "xl", "core")
    )
    placed = (P(DEPTH, ROW, "z"), P("z", ROW), P(), P(), P())
    return jax.shard_map(
        shards,
        mesh=fine,
        in_specs=placed,
        out_specs=P(("y", "xh", "xl", "core"), "z"),
        check_vma=False,
    )
```

time: 1920 us -> 99.3 us (0.05)
  the two profiles are of different devices: /device:TPU:1 before, /device:TPU:59 now
where the time goes in v1:
time: 99.3 us; the launch traced here: 98.9 us
  blocking collectives  33.7 us (34%)
  starting transfers between devices  22 us (22%)
  waiting for transfers between devices  18.1 us (18%)
  between operations  13.5 us (14%)
  Pallas kernels  9.61 us (10%)
  local copies, waits for them, and re-layouts  1.83 us (2%)
    all_gather x1, blocking collectives, shards(): rows_in = lax.all_gather(rows_out, PLANE)  20.3 us
    ppermute x3, waiting for transfers between devices, shards(): top_panel = top_panel + lax.ppermute(top_panel, 'y', pairs)  16.4 us
    all_to_all x1, blocking collectives, shards(): got = lax.all_to_all(send, PLANE, 0, 0)  13.3 us
    all_to_all x1, starting transfers between devices, shards(): panel_p = lax.all_to_all(panel_out, 'z', 0, 0)  9.61 us
    all_to_all x1, starting transfers between devices, shards(): got = lax.all_to_all(send, 'y', 0, 0)  6.74 us
    pallas_call x1, Pallas kernels, shards(): pl.pallas_call(pivot_kernel, out_shape=(jax.ShapeDtypeStruct((n_plane, 2...  3.76 us
    pallas_call x1, Pallas kernels, shards(): pl.pallas_call(update_kernel, out_shape=jax.ShapeDtypeStruct((share, colu...  3.2 us
    ppermute x1, starting transfers between devices, shards(): top_panel = top_panel + lax.ppermute(top_panel, 'xh', [(0, 1)])  3.07 us
  transfers between devices with their start and end apart: 7, of which 2 were waited for; matrix products, arithmetic and copies ran while one was open for 0% of the time, Pallas kernels for 6%

profile of v1, /device:TPU:59, one launch (start us, length us, event | category | flops | bytes accessed | tf_op | source)
XLA Modules:
  0.0 98.9 jit_solution(7100803909194537753)
XLA Ops:
  6.5 0.0 copy-start
  6.5 0.0 copy-start.5
  6.5 0.0 reduce-scatter.2.cloned.1.call-start
  6.5 0.7 reduce-scatter.2.cloned.1.call-update
  7.3 0.1 pad_add_fusion.place
  7.3 0.8 copy-done
  8.1 0.0 copy-done.5
  8.1 3.8 %pivot_rows.1 = (f32[8,64,256]{2,1,0:T(8,128)S(1)}, s32[1,512]{1,0:T(1,128)S(1)}, s32[512,128]{1,0:T(8,128)S(1)}) custom-call(s32[3]{0:T(128)S(1)} %pad_add_fusion.place, s32[1,256]{1,0:T(1,128)S(1)} %bitcast.9, f32[2048,256]{1,0:T(8,128)S(1)} %bitcast.7), custom_call_target="tpu_custom_call" | custom-call | tf_op jit(solution)/shard_map/pivot_rows/pallas_call | solution.py:182
  11.9 0.0 copy-start.2
  11.9 13.3 %all_to_all.15.got = f32[8,64,256]{2,1,0:T(8,128)S(1)} all-to-all(f32[8,64,256]{2,1,0:T(8,128)S(1)} %get-tuple-element.10), channel_id=1, replica_groups=mesh['y'=8,'xh'=2,'z'=8,'xl'=2,'core'=2] {'xh','xl','core'}, dimensions={0} | all-to-all | bytes 1048576 | tf_op jit(solution)/shard_map/all_to_all | solution.py:209
  25.2 0.8 plane_sum.1
  26.1 0.0 copy-start.4
  26.1 6.7 %all-to-all-start.1 = ((f32[8,64,256]{2,1,0:T(8,128)}), f32[8,64,256]{2,1,0:T(8,128)S(1)}, u32[]{:S(2)}, u32[]{:S(2)}) async-start(f32[8,64,256]{2,1,0:T(8,128)} %plane_sum.1), calls=%async_computation.2 | async-start | bytes 1048576 | tf_op jit(solution)/shard_map/all_to_all | solution.py:218
  32.8 0.0 copy-done.2
  32.8 0.7 collective-permute-start
  33.5 0.0 collective-permute-done
  33.5 0.7 collective-permute-start.1
  34.2 0.0 collective-permute-done.1
  34.2 1.3 %collective-permute-start.2 = (f32[32,256]{1,0:T(8,128)S(1)}, f32[32,256]{1,0:T(8,128)S(1)}, u32[]{:S(2)}, u32[]{:S(2)}) collective-permute-start(f32[32,256]{1,0:T(8,128)S(1)} %add.27), channel_id=1, source_target_pairs={{0,64},{128,192},{256,320},{384,448},{1,65},{129,193},{257,321},{3... | collective-permute-start | bytes 98312 | tf_op jit(solution)/shard_map/ppermute | solution.py:205
  35.5 16.4 %collective-permute-done.2 = f32[32,256]{1,0:T(8,128)S(1)} collective-permute-done((f32[32,256]{1,0:T(8,128)S(1)}, f32[32,256]{1,0:T(8,128)S(1)}, u32[]{:S(2)}, u32[]{:S(2)}) %collective-permute-start.2) | collective-permute-done | bytes 32800 | tf_op jit(solution)/shard_map/ppermute | solution.py:205
  51.9 3.1 %collective-permute-start.3 = (f32[32,256]{1,0:T(8,128)S(1)}, f32[32,256]{1,0:T(8,128)S(1)}, u32[]{:S(2)}, u32[]{:S(2)}) collective-permute-start(f32[32,256]{1,0:T(8,128)S(1)} %add.28), channel_id=1, source_target_pairs={{0,32},{1,33},{2,34},{3,35},{4,36},{5,37},{6,38},{7,39},{8,40},{9,... | collective-permute-start | bytes 98312 | tf_op jit(solution)/shard_map/ppermute | solution.py:207
  55.0 1.0 %collective-permute-done.3 = f32[32,256]{1,0:T(8,128)S(1)} collective-permute-done((f32[32,256]{1,0:T(8,128)S(1)}, f32[32,256]{1,0:T(8,128)S(1)}, u32[]{:S(2)}, u32[]{:S(2)}) %collective-permute-start.3) | collective-permute-done | bytes 32800 | tf_op jit(solution)/shard_map/ppermute | solution.py:207
  56.0 0.0 all-to-all-done.1.got
  56.0 1.8 %column_sum.1 = (f32[64,256]{1,0:T(8,128)S(1)}, f32[8,32,512]{2,1,0:T(8,128)}) custom-call(s32[3]{0:T(128)S(1)} %pad_add_fusion.place, f32[8,64,256]{2,1,0:T(8,128)S(1)} %all-to-all-done.1.got, f32[32,2048]{1,0:T(8,128)S(1)} %copy-done.2, f32[32,256]{1,0:T(8,128)S(1)} %add.29.top_panel, s32[1,512]{1,0:T(1,128)S(1)} %get-tuple-element.11.top_row), custom_call_target="tpu_custom_call" | custom-call | tf_op jit(solution)/shard_map/column_sum/pallas_call | solution.py:219
  57.8 9.6 %all-to-all-start.2 = ((f32[8,32,512]{2,1,0:T(8,128)}), f32[8,32,512]{2,1,0:T(8,128)S(1)}, u32[]{:S(2)}, u32[]{:S(2)}) async-start(f32[8,32,512]{2,1,0:T(8,128)} %get-tuple-element.12), calls=%async_computation.3 | async-start | bytes 1048576 | tf_op jit(solution)/shard_map/all_to_all | solution.py:230
  67.4 20.3 %all-gather = f32[512,256]{1,0:T(8,128)S(1)} all-gather(f32[64,256]{1,0:T(8,128)S(1)} %get-tuple-element.13), channel_id=2, replica_groups=mesh['y'=8,'xh'=2,'z'=8,'xl'=2,'core'=2] {'xh','xl','core'}, dimensions={0}, use_global_device_ids=true | all-gather | bytes 589824 | tf_op jit(solution)/shard_map/all_gather | solution.py:231
  87.7 0.0 all-to-all-done.2.panel
  87.8 0.0 copy-done.3
  87.8 0.0 copy-done.4
  87.8 0.0 copy-start.1
  87.8 1.0 %copy-done.1 = f32[512,256]{1,0:T(8,128)S(1)} copy-done((f32[512,256]{1,0:T(8,128)S(1)}, f32[512,256]{1,0:T(8,128)}, u32[]{:S(2)}) %copy-start.1) | copy-done | bytes 524312
  88.8 3.2 %update_rows.1 = f32[512,256]{1,0:T(8,128)} custom-call(s32[3]{0:T(128)S(1)} %pad_add_fusion.place, f32[512,256]{1,0:T(8,128)S(1)} %copy-done.1, f32[8,32,512]{2,1,0:T(8,128)S(1)} %all-to-all-done.2.panel, f32[8,64,256]{2,1,0:T(8,128)S(1)} %bitcast.8, f32[256,256]{1,0:T(8,128)S(1)} %copy-done.3, f32[256,256]{1,0:T(8,128)S(1)} %copy-done.4, ...), custom_call_target="tpu_custom_call" | custom-call | tf_op jit(solution)/shard_map/update_rows/pallas_call | solution.py:232
  (7 shorter events, 0.0 us)
Async XLA Ops:
  6.5 1.6 %copy-start = (f32[1,2048,256]{2,1,0:T(8,128)S(1)}, f32[1,2048,256]{2,1,0:T(8,128)}, u32[]{:S(2)}) copy-start(f32[1,2048,256]{2,1,0:T(8,128)} %param.5) | copy-start | bytes 6291460
  6.5 1.6 %copy-start.5 = (s32[256]{0:T(256)S(1)}, s32[256]{0:T(256)}, u32[]{:S(2)}) copy-start(s32[256]{0:T(256)} %param.9) | copy-start | bytes 3076
  6.5 81.2 %reduce-scatter.2.cloned.1.call-start = ((), (), s32[]{:S(2)}) async-start(), calls=%async_computation.4 | async-start | bytes 2621440 | tf_op jit(solution)/shard_map/reduce_scatter | solution.py:180
  11.9 20.9 %copy-start.2 = (f32[32,2048]{1,0:T(8,128)S(1)}, f32[32,2048]{1,0:T(8,128)}, u32[]{:S(2)}) copy-start(f32[32,2048]{1,0:T(8,128)} %panel.1) | copy-start | bytes 786436
  26.1 61.7 %copy-start.3 = (f32[256,256]{1,0:T(8,128)S(1)}, f32[256,256]{1,0:T(8,128)}, u32[]{:S(2)}) copy-start(f32[256,256]{1,0:T(8,128)} %l_inv.1) | copy-start | bytes 786436
  26.1 61.7 %copy-start.4 = (f32[256,256]{1,0:T(8,128)S(1)}, f32[256,256]{1,0:T(8,128)}, u32[]{:S(2)}) copy-start(f32[256,256]{1,0:T(8,128)} %u_inv.1) | copy-start | bytes 786436
  26.1 29.9 %all-to-all-start.1 = ((f32[8,64,256]{2,1,0:T(8,128)}), f32[8,64,256]{2,1,0:T(8,128)S(1)}, u32[]{:S(2)}, u32[]{:S(2)}) async-start(f32[8,64,256]{2,1,0:T(8,128)} %plane_sum.1), calls=%async_computation.2 | async-start | bytes 1048576 | tf_op jit(solution)/shard_map/all_to_all | solution.py:218
  32.8 0.7 collective-permute-start
  33.5 0.7 collective-permute-start.1
  34.2 17.7 %collective-permute-start.2 = (f32[32,256]{1,0:T(8,128)S(1)}, f32[32,256]{1,0:T(8,128)S(1)}, u32[]{:S(2)}, u32[]{:S(2)}) collective-permute-start(f32[32,256]{1,0:T(8,128)S(1)} %add.27), channel_id=1, source_target_pairs={{0,64},{128,192},{256,320},{384,448},{1,65},{129,193},{257,321},{3... | collective-permute-start | bytes 98312 | tf_op jit(solution)/shard_map/ppermute | solution.py:205
  51.9 4.1 %collective-permute-start.3 = (f32[32,256]{1,0:T(8,128)S(1)}, f32[32,256]{1,0:T(8,128)S(1)}, u32[]{:S(2)}, u32[]{:S(2)}) collective-permute-start(f32[32,256]{1,0:T(8,128)S(1)} %add.28), channel_id=1, source_target_pairs={{0,32},{1,33},{2,34},{3,35},{4,36},{5,37},{6,38},{7,39},{8,40},{9,... | collective-permute-start | bytes 98312 | tf_op jit(solution)/shard_map/ppermute | solution.py:207
  57.8 29.9 %all-to-all-start.2 = ((f32[8,32,512]{2,1,0:T(8,128)}), f32[8,32,512]{2,1,0:T(8,128)S(1)}, u32[]{:S(2)}, u32[]{:S(2)}) async-start(f32[8,32,512]{2,1,0:T(8,128)} %get-tuple-element.12), calls=%async_computation.3 | async-start | bytes 1048576 | tf_op jit(solution)/shard_map/all_to_all | solution.py:230
  87.8 1.0 %copy-start.1 = (f32[512,256]{1,0:T(8,128)S(1)}, f32[512,256]{1,0:T(8,128)}, u32[]{:S(2)}) copy-start(f32[512,256]{1,0:T(8,128)} %reduce-scatter.2.cloned.1.call-done.slab) | copy-start | bytes 1572868
Sparse Core Ops, SparseCore 0:
  10.2 36.8 reduce-scatter.1

commit v2 on v1

--- a/solution.py
+++ b/solution.py
@@ -14,9 +14,9 @@
 HIGHEST = lax.Precision.HIGHEST
 F32 = jnp.float32
 I32 = jnp.int32
+ANY = pl.BlockSpec(memory_space=pl.ANY)
 VMEM = pl.BlockSpec(memory_space=pltpu.VMEM)
 SMEM = pl.BlockSpec(memory_space=pltpu.SMEM)
-ANY = pl.BlockSpec(memory_space=pl.ANY)
 
 
 def lane_lookup(table, index):
@@ -33,16 +33,31 @@
     return jnp.concatenate(parts, axis=1)
 
 
-def pivot_kernel(place, pivots, slab_hbm, send, top_row, top_col, slab, source_v, source_s, sems):
+def top_kernel(slab, panel, send, sems, *, layers):
+    groups, both, _ = send.shape
+    fill = panel.shape[0] // layers
+    block = both - fill
+    width = groups * block
+    start = pl.multiple_of(lax.axis_index(DEPTH) * fill, fill)
+    copies = []
+    for target in range(groups):
+        rows = slab.at[pl.ds(target * block, block), :]
+        part = panel.at[pl.ds(start, fill), pl.ds(0, width)]
+        copies.append(pltpu.make_async_copy(rows, send.at[target, pl.ds(0, block)], sems.at[0, target]))
+        copies.append(pltpu.make_async_copy(part, send.at[target, pl.ds(block, fill)], sems.at[1, target]))
+    for copy in copies:
+        copy.start()
+    for copy in copies:
+        copy.wait()
+
+
+def pivot_kernel(place, pivots, slab, send, top_row, top_col, give, source_v, source_s, sem):
     rows, columns = slab.shape
     width = pivots.shape[1]
-    groups, both, _ = send.shape
-    block = both // 2
+    groups, block, _ = send.shape
     share = top_row.shape[1]
     row_start = place[0]
     share_start = place[1]
-    fetch = pltpu.make_async_copy(slab_hbm, slab, sems.at[0])
-    fetch.start()
     along = lax.broadcasted_iota(I32, (width, width), 1)
     down = lax.broadcasted_iota(I32, (width, width), 0)
     pivot_row = pivots[...]
@@ -67,7 +82,7 @@
         lane_lookup(content, jnp.maximum(last, 0)),
     )
     source_v[...] = source
-    to_scalar = pltpu.make_async_copy(source_v, source_s, sems.at[1])
+    to_scalar = pltpu.make_async_copy(source_v, source_s, sem)
     to_scalar.start()
     content_row = content[:1]
     target_row = jnp.where((later == 0) & (pivot_row >= width), pivot_row, -1)
@@ -86,9 +101,9 @@
     own_down = share_start + lax.broadcasted_iota(I32, (share, width), 0)
     found = jnp.max(jnp.where(target_row == own_down, content_row, -1), axis=1, keepdims=True)
     top_col[...] = jnp.broadcast_to(found, top_col.shape)
-    fetch.wait()
-    for group in range(groups):
-        send[group, block:, :] = slab[group * block : (group + 1) * block, :]
+    for half in range(give.shape[0]):
+        start = pl.multiple_of((2 * half + place[3]) * share, share)
+        give[half] = slab[pl.ds(start, share), :]
     to_scalar.wait()
 
     def gather(group, carry):
@@ -103,29 +118,33 @@
     lax.fori_loop(0, groups, gather, 0)
 
 
-def plane_sum_kernel(got, send):
-    groups, both, _ = got.shape
-    block = both // 2
+def pack_kernel(moved, got, send):
+    groups, block, _ = moved.shape
+    part = send.shape[1] - got.shape[1]
+    for target in range(groups):
+        send[target, :block, :] = moved[target]
+    fill = got.shape[1] - block
+    for target in range(groups):
+        send[target, block : block + fill, :] = got[0, block:, :]
+        send[target, block + fill :, :] = got[0, target * part : (target + 1) * part, :]
+
+
+def plane_sum_kernel(place, got, panel, top_row, send, panel_out, top_panel, *, block):
+    groups = got.shape[0]
     first = groups // 2
+    part = send.shape[1] - block
+    fill = got.shape[1] - block - part
     moved = got[0, :block, :]
     for source in range(1, groups):
         moved = moved + got[source, :block, :]
-    top = got[0, block:, :]
+    top = got[0, block + fill :, :]
     for source in range(1, first):
-        top = top + got[source, block:, :]
+        top = top + got[source, block + fill :, :]
     for target in range(send.shape[0]):
         send[target, :block, :] = moved
         send[target, block:, :] = top
-
-
-def column_kernel(place, got, panel, top_panel, top_row, rows_out, panel_out):
-    groups, both, _ = got.shape
-    block = both // 2
-    moved = got[0, :block, :]
-    for source in range(1, groups):
-        moved = moved + got[source, :block, :]
-    rows_out[:block, :] = moved
-    rows_out[block:, :] = got[0, block:, :]
+    for source in range(first):
+        top_panel[source * fill : (source + 1) * fill, :] = got[source, block : block + fill, :]
     share = top_row.shape[1]
     width = top_panel.shape[1]
     lands = top_row[...]
@@ -133,14 +152,27 @@
     chosen = jnp.where(slot == lands, 1.0, 0.0).astype(F32)
     replaced = jnp.dot(top_panel[...], chosen, precision=HIGHEST, preferred_element_type=F32)
     own = panel[:, pl.ds(pl.multiple_of(place[2] * share, share), share)]
-    fixed = jnp.where(lands >= 0, replaced, own)
+    panel_out[...] = jnp.where(lands >= 0, replaced, own)
+
+
+def column_kernel(got, panel, rows_out, panel_out):
+    groups, both, _ = got.shape
+    block = rows_out.shape[0] // 2
+    part = both - block
+    moved = got[0, :block, :]
+    for source in range(1, groups):
+        moved = moved + got[source, :block, :]
+    rows_out[:block, :] = moved
+    for source in range(groups):
+        rows_out[block + source * part : block + (source + 1) * part, :] = got[source, block:, :]
     for target in range(panel_out.shape[0]):
-        panel_out[target] = fixed
-
-
-def update_kernel(place, slab, panel, rows_in, l_inv, u_inv, top_col, out):
+        panel_out[target] = panel[...]
+
+
+def update_kernel(place, slab, slab_got, panel, rows_in, l_inv, u_inv, top_col, out, *, n_y):
     groups, both, columns = rows_in.shape
     block = both // 2
+    part = block // n_y
     width = l_inv.shape[0]
     share = slab.shape[0]
     panel_p = panel[...].reshape(width, share)
@@ -152,9 +184,11 @@
     upper = jnp.dot(l_inv[...], moved, precision=HIGHEST, preferred_element_type=F32)
     lands = top_col[:, :1]
     slot = lax.broadcasted_iota(I32, (share, width), 1)
-    chosen = jnp.where(slot == lands, 1.0, 0.0).astype(F32)
+    member, rest = slot // block, slot % block
+    holds = (rest // part) * (groups * part) + member * part + rest % part
+    chosen = jnp.where(holds == lands, 1.0, 0.0).astype(F32)
     replaced = jnp.dot(chosen, top, precision=HIGHEST, preferred_element_type=F32)
-    slab_p = jnp.where(lands >= 0, replaced, slab[...])
+    slab_p = jnp.where(lands >= 0, replaced, slab[...] + slab_got[...])
     out[...] = slab_p - jnp.dot(lower, upper, precision=HIGHEST, preferred_element_type=F32)
 
     @pl.when(place[1] == 0)
@@ -172,71 +206,105 @@
     n_plane = lax.axis_size(PLANE)
     share = rows // n_depth
     block = width // n_plane
+    part = block // n_y
+    fill = tall // n_depth
     row_index = lax.axis_index(ROW)
     layer = lax.axis_index(DEPTH)
+    x_index = lax.axis_index("xl")
+    core = lax.axis_index("core")
     row_start = row_index * rows
-    place = jnp.stack([row_start, row_start + layer * share, layer]).astype(I32)
-
-    slab_sum = lax.psum_scatter(slab_local, DEPTH, scatter_dimension=0, tiled=True)
-
-    send, top_row, top_col = pl.pallas_call(
+    place = jnp.stack([row_start, row_start + layer * share, layer, 1 - core]).astype(I32)
+    swap = [(0, 1), (1, 0)]
+    params = pltpu.CompilerParams(vmem_limit_bytes=32 << 20)
+
+    wide = pltpu.CompilerParams(vmem_limit_bytes=56 << 20)
+
+    top = pl.pallas_call(
+        functools.partial(top_kernel, layers=n_depth),
+        out_shape=jax.ShapeDtypeStruct((n_y, width // n_y + fill, columns), F32),
+        in_specs=[ANY, ANY],
+        out_specs=VMEM,
+        scratch_shapes=[pltpu.SemaphoreType.DMA((2, n_y))],
+        compiler_params=wide,
+        name="top_rows",
+    )(slab_local, panel_t)
+    top, place = lax.optimization_barrier((top, place))
+    top = lax.all_to_all(top, "y", 0, 0)
+
+    moved, top_row, top_col, give = pl.pallas_call(
         pivot_kernel,
         out_shape=(
-            jax.ShapeDtypeStruct((n_plane, 2 * block, columns), F32),
+            jax.ShapeDtypeStruct((n_plane, block, columns), F32),
             jax.ShapeDtypeStruct((1, share), I32),
             jax.ShapeDtypeStruct((share, 128), I32),
+            jax.ShapeDtypeStruct((n_depth // 2, share, columns), F32),
         ),
-        in_specs=[SMEM, VMEM, ANY],
-        out_specs=(VMEM, VMEM, VMEM),
+        in_specs=[SMEM, VMEM, VMEM],
+        out_specs=(VMEM, VMEM, VMEM, VMEM),
         scratch_shapes=[
-            pltpu.VMEM((rows, columns), F32),
             pltpu.VMEM((8, width), I32),
             pltpu.SMEM((8, width), I32),
-            pltpu.SemaphoreType.DMA((2,)),
+            pltpu.SemaphoreType.DMA,
         ],
-        compiler_params=pltpu.CompilerParams(vmem_limit_bytes=32 << 20),
+        compiler_params=params,
+        cost_estimate=pl.CostEstimate(
+            flops=2 * width * rows * columns, bytes_accessed=16 * rows * columns, transcendentals=0
+        ),
         name="pivot_rows",
     )(place, pivots.reshape(1, width), slab_local)
 
-    top_panel = jnp.where(row_index == 0, panel_t[:, :width], 0.0)
-    step = n_y // 2
-    while step >= 1:
-        pairs = [(at, at + step) for at in range(0, n_y, 2 * step)]
-        top_panel = top_panel + lax.ppermute(top_panel, "y", pairs)
-        step //= 2
-    top_panel = top_panel + lax.ppermute(top_panel, "xh", [(0, 1)])
-
+    send = pl.pallas_call(
+        pack_kernel,
+        out_shape=jax.ShapeDtypeStruct((n_plane, block + fill + part, columns), F32),
+        in_specs=[VMEM, VMEM],
+        out_specs=VMEM,
+        compiler_params=params,
+        name="pack_plane",
+    )(moved, top)
+    send, give = lax.optimization_barrier((send, give))
+    core_got = lax.ppermute(give, "core", swap)
+    by_core = slab_local.reshape(n_depth // 2, 2, share, columns)
+    half = lax.dynamic_index_in_dim(by_core, core, 1, keepdims=False) + core_got
+    slab_own = lax.dynamic_index_in_dim(half, x_index, 0, keepdims=False)
+    slab_give = lax.dynamic_index_in_dim(half, 1 - x_index, 0, keepdims=False)
     got = lax.all_to_all(send, PLANE, 0, 0)
-    send = pl.pallas_call(
-        plane_sum_kernel,
-        out_shape=jax.ShapeDtypeStruct((n_y, 2 * block, columns), F32),
-        in_specs=[VMEM],
-        out_specs=VMEM,
-        compiler_params=pltpu.CompilerParams(vmem_limit_bytes=32 << 20),
+    send, panel_own = pl.pallas_call(
+        functools.partial(plane_sum_kernel, block=block),
+        out_shape=(
+            jax.ShapeDtypeStruct((n_y, block + part, columns), F32),
+            jax.ShapeDtypeStruct((tall, share), F32),
+        ),
+        in_specs=[SMEM, VMEM, VMEM, VMEM],
+        out_specs=(VMEM, VMEM),
+        scratch_shapes=[pltpu.VMEM((tall, width), F32)],
+        compiler_params=params,
         name="plane_sum",
-    )(got)
+    )(place, got, panel_t, top_row)
+    send, slab_own, slab_give = lax.optimization_barrier((send, slab_own, slab_give))
+    slab_got = lax.ppermute(slab_give, "xl", swap)
     got = lax.all_to_all(send, "y", 0, 0)
+    got, slab_got = lax.optimization_barrier((got, slab_got))
     rows_out, panel_out = pl.pallas_call(
         column_kernel,
         out_shape=(
             jax.ShapeDtypeStruct((2 * block, columns), F32),
             jax.ShapeDtypeStruct((n_z, tall, share), F32),
         ),
-        in_specs=[SMEM, VMEM, VMEM, VMEM, VMEM],
+        in_specs=[VMEM, VMEM],
         out_specs=(VMEM, VMEM),
-        compiler_params=pltpu.CompilerParams(vmem_limit_bytes=32 << 20),
+        compiler_params=params,
         name="column_sum",
-    )(place, got, panel_t, top_panel, top_row)
+    )(got, panel_own)
     panel_p = lax.all_to_all(panel_out, "z", 0, 0)
     rows_in = lax.all_gather(rows_out, PLANE)
     return pl.pallas_call(
-        update_kernel,
+        functools.partial(update_kernel, n_y=n_y),
         out_shape=jax.ShapeDtypeStruct((share, columns), F32),
-        in_specs=[SMEM, VMEM, VMEM, VMEM, VMEM, VMEM, VMEM],
+        in_specs=[SMEM] + [VMEM] * 7,
         out_specs=VMEM,
-        compiler_params=pltpu.CompilerParams(vmem_limit_bytes=32 << 20),
+        compiler_params=params,
         name="update_rows",
-    )(place, slab_sum, panel_p, rows_in, l_inv, u_inv, top_col)
+    )(place, slab_own, slab_got, panel_p, rows_in, l_inv, u_inv, top_col)
 
 
 def solution(mesh):

time: 99.3 us -> 89.1 us (0.90)
  the two profiles are of different devices: /device:TPU:59 before, /device:TPU:1 now
where the time goes in v2:
time: 89.1 us; the launch traced here: 87.8 us
  starting transfers between devices  30.5 us (34%)
  blocking collectives  29.8 us (33%)
  waiting for transfers between devices  13.5 us (15%)
  Pallas kernels  11.4 us (13%)
  other arithmetic  1.45 us (2%)
  local copies, waits for them, and re-layouts  1.08 us (1%)
    all_gather x1, blocking collectives, shards(): rows_in = lax.all_gather(rows_out, PLANE)  16.2 us
    all_to_all x1, blocking collectives, shards(): got = lax.all_to_all(send, 'y', 0, 0)  13.6 us
    all_to_all x1, starting transfers between devices, shards(): panel_p = lax.all_to_all(panel_out, 'z', 0, 0)  10 us
    all_to_all x1, waiting for transfers between devices, shards(): got = lax.all_to_all(send, PLANE, 0, 0)  8.08 us
    all_to_all x1, starting transfers between devices, shards(): top = lax.all_to_all(top, 'y', 0, 0)  7.65 us
    ppermute x1, starting transfers between devices, shards(): core_got = lax.ppermute(give, 'core', swap)  6.06 us
    all_to_all x1, waiting for transfers between devices, shards(): top = lax.all_to_all(top, 'y', 0, 0)  5.45 us
    all_to_all x1, starting transfers between devices, shards(): got = lax.all_to_all(send, PLANE, 0, 0)  4.42 us
  transfers between devices with their start and end apart: 5, of which 2 were waited for; matrix products, arithmetic and copies ran while one was open for 0% of the time, Pallas kernels for 5%

profile of v2, /device:TPU:1, one launch (start us, length us, event | category | flops | bytes accessed | tf_op | source)
XLA Modules:
  0.0 87.8 jit_solution(6082736026293026407)
XLA Ops:
  0.0 0.0 copy-start
  0.0 0.0 copy-start.4
  0.0 1.9 %top_rows.1 = f32[8,40,256]{2,1,0:T(8,128)} custom-call(f32[2048,256]{1,0:T(8,128)} %bitcast.16, f32[32,2048]{1,0:T(8,128)} %panel.3), custom_call_target="tpu_custom_call" | custom-call | tf_op jit(solution)/shard_map/top_rows/pallas_call | solution.py:222
  1.9 0.1 pad_add_fusion.place
  2.0 7.7 %all-to-all-start = ((f32[8,40,256]{2,1,0:T(8,128)}), f32[8,40,256]{2,1,0:T(8,128)S(1)}, u32[]{:S(2)}, u32[]{:S(2)}) async-start(f32[8,40,256]{2,1,0:T(8,128)} %top_rows.1), calls=%async_computation | async-start | bytes 655360 | tf_op jit(solution)/shard_map/all_to_all | solution.py:232
  9.7 0.0 copy-done
  9.7 0.0 copy-done.4
  9.7 3.6 %pivot_rows.1 = (f32[8,32,256]{2,1,0:T(8,128)S(1)}, s32[1,512]{1,0:T(1,128)S(1)}, s32[512,128]{1,0:T(8,128)S(1)}, f32[2,512,256]{2,1,0:T(8,128)S(1)}) custom-call(s32[4]{0:T(128)S(1)} %pad_add_fusion.place, s32[1,256]{1,0:T(1,128)S(1)} %bitcast.20, f32[2048,256]{1,0:T(8,128)S(1)} %bitcast.17), custom_call_target="tpu_custom_call" | custom-call | flops 268435456 | bytes 8388608 | tf_op jit(solution)/shard_map/pivot_rows/pallas_call | solution.py:234
  13.3 0.0 copy-start.5
  13.3 1.0 %copy-done.5 = f32[2,512,256]{2,1,0:T(8,128)} copy-done((f32[2,512,256]{2,1,0:T(8,128)}, f32[2,512,256]{2,1,0:T(8,128)S(1)}, u32[]{:S(2)}) %copy-start.5) | copy-done | bytes 1048600
  14.3 5.4 %all-to-all-done.got = f32[8,40,256]{2,1,0:T(8,128)S(1)} async-done(((f32[8,40,256]{2,1,0:T(8,128)}), f32[8,40,256]{2,1,0:T(8,128)S(1)}, u32[]{:S(2)}, u32[]{:S(2)}) %all-to-all-start) | async-done | bytes 327712 | tf_op jit(solution)/shard_map/all_to_all | solution.py:232
  19.8 0.8 pack_plane.1
  20.5 6.1 %collective-permute-start = (f32[2,512,256]{2,1,0:T(8,128)}, f32[2,512,256]{2,1,0:T(8,128)}, u32[]{:S(2)}, u32[]{:S(2)}) collective-permute-start(f32[2,512,256]{2,1,0:T(8,128)} %copy-done.5), channel_id=1, source_target_pairs={{0,1},{1,0},{2,3},{3,2},{4,5},{5,4},{6,7},{7,6},{8,9},{9,8},{10,11... | collective-permute-start | bytes 3145736 | tf_op jit(solution)/shard_map/ppermute | solution.py:265
  26.6 4.4 %all-to-all-start.1 = ((f32[8,44,256]{2,1,0:T(8,128)}), f32[8,44,256]{2,1,0:T(8,128)S(1)}, u32[]{:S(2)}, u32[]{:S(2)}) async-start(f32[8,44,256]{2,1,0:T(8,128)} %pack_plane.1), calls=%async_computation.1 | async-start | bytes 786432 | tf_op jit(solution)/shard_map/all_to_all | solution.py:270
  31.0 8.1 %all-to-all-done.1.got = f32[8,44,256]{2,1,0:T(8,128)S(1)} async-done(((f32[8,44,256]{2,1,0:T(8,128)}), f32[8,44,256]{2,1,0:T(8,128)S(1)}, u32[]{:S(2)}, u32[]{:S(2)}) %all-to-all-start.1) | async-done | bytes 360480 | tf_op jit(solution)/shard_map/all_to_all | solution.py:270
  39.1 0.0 copy-done.1
  39.1 1.0 %plane_sum.1 = (f32[8,36,256]{2,1,0:T(8,128)S(1)}, f32[32,512]{1,0:T(8,128)S(1)}) custom-call(s32[4]{0:T(128)S(1)} %pad_add_fusion.place, f32[8,44,256]{2,1,0:T(8,128)S(1)} %all-to-all-done.1.got, f32[32,2048]{1,0:T(8,128)S(1)} %copy-done.1, s32[1,512]{1,0:T(1,128)S(1)} %get-tuple-element.27.top_row), custom_call_target="tpu_custom_call" | custom-call | tf_op jit(solution)/shard_map/plane_sum/pallas_call | solution.py:271
  40.1 0.0 collective-permute-done
  40.1 1.4 %bitcast_add_fusion = f32[2,512,256]{2,1,0:T(8,128)S(1)} fusion(f32[2,512,256]{2,1,0:T(8,128)} %collective-permute-done, f32[2,2,512,256]{3,2,1,0:T(8,128)S(1)} %bitcast.18, s32[]{:T(128)S(6)} %select_n.11), kind=kLoop, calls=%fused_computation | loop fusion | flops 262144 | bytes 3145732 | tf_op jit(solution)/shard_map/add | solution.py:267
  41.5 0.0 copy-start.2
  41.5 0.0 copy-start.3
  41.5 0.1 dynamic-slice_bitcast_fusion
  41.6 2.3 %collective-permute-start.1 = (f32[512,256]{1,0:T(8,128)S(1)}, f32[512,256]{1,0:T(8,128)S(1)}, u32[]{:S(2)}, u32[]{:S(2)}) collective-permute-start(f32[512,256]{1,0:T(8,128)S(1)} %get-tuple-element.32), channel_id=1, source_target_pairs={{0,2},{2,0},{1,3},{3,1},{4,6},{6,4},{5,7},{7,5},{8,10},{10,8},{9,1... | collective-permute-start | bytes 1572872 | tf_op jit(solution)/shard_map/ppermute | solution.py:284
  43.9 13.6 %all_to_all.20.got = f32[8,36,256]{2,1,0:T(8,128)S(1)} all-to-all(f32[8,36,256]{2,1,0:T(8,128)S(1)} %get-tuple-element.31), channel_id=1, replica_groups=mesh['y'=8,'xh'=2,'z'=8,'xl'=2,'core'=2] {'y'}, dimensions={0} | all-to-all | bytes 589824 | tf_op jit(solution)/shard_map/all_to_all | solution.py:285
  57.6 0.0 collective-permute-done.1.slab_got
  57.6 0.8 column_sum.1
  58.4 10.0 %all-to-all-start.3 = ((f32[8,32,512]{2,1,0:T(8,128)}), f32[8,32,512]{2,1,0:T(8,128)S(1)}, u32[]{:S(2)}, u32[]{:S(2)}) async-start(f32[8,32,512]{2,1,0:T(8,128)} %get-tuple-element.36), calls=%async_computation.3 | async-start | bytes 1048576 | tf_op jit(solution)/shard_map/all_to_all | solution.py:298
  68.4 16.2 %all-gather = f32[512,256]{1,0:T(8,128)S(1)} all-gather(f32[64,256]{1,0:T(8,128)S(1)} %get-tuple-element.37), channel_id=2, replica_groups=mesh['y'=8,'xh'=2,'z'=8,'xl'=2,'core'=2] {'xh','xl','core'}, dimensions={0}, use_global_device_ids=true | all-gather | bytes 589824 | tf_op jit(solution)/shard_map/all_gather | solution.py:299
  84.6 0.0 all-to-all-done.3.panel
  84.6 0.0 copy-done.2
  84.6 0.0 copy-done.3
  84.6 3.2 %update_rows.1 = f32[512,256]{1,0:T(8,128)} custom-call(s32[4]{0:T(128)S(1)} %pad_add_fusion.place, f32[512,256]{1,0:T(8,128)S(1)} %get-tuple-element.30.slab, f32[512,256]{1,0:T(8,128)S(1)} %collective-permute-done.1.slab_got, f32[8,32,512]{2,1,0:T(8,128)S(1)} %all-to-all-done.3.panel, f32[8,64,256]{2,1,0:T(8,128)S(1)} %bitcast.19, ...), custom_call_target="tpu_custom_call" | custom-call | tf_op jit(solution)/shard_map/update_rows/pallas_call | solution.py:300
  (1 shorter events, 0.0 us)
Async XLA Ops:
  0.0 9.7 %copy-start = (f32[1,2048,256]{2,1,0:T(8,128)S(1)}, f32[1,2048,256]{2,1,0:T(8,128)}, u32[]{:S(2)}) copy-start(f32[1,2048,256]{2,1,0:T(8,128)} %param.5) | copy-start | bytes 6291460
  0.0 9.7 %copy-start.4 = (s32[256]{0:T(256)S(1)}, s32[256]{0:T(256)}, u32[]{:S(2)}) copy-start(s32[256]{0:T(256)} %param.9) | copy-start | bytes 3076
  2.0 17.7 %all-to-all-start = ((f32[8,40,256]{2,1,0:T(8,128)}), f32[8,40,256]{2,1,0:T(8,128)S(1)}, u32[]{:S(2)}, u32[]{:S(2)}) async-start(f32[8,40,256]{2,1,0:T(8,128)} %top_rows.1), calls=%async_computation | async-start | bytes 655360 | tf_op jit(solution)/shard_map/all_to_all | solution.py:232
  9.7 29.4 %copy-start.1 = (f32[32,2048]{1,0:T(8,128)S(1)}, f32[32,2048]{1,0:T(8,128)}, u32[]{:S(2)}) copy-start(f32[32,2048]{1,0:T(8,128)} %panel.3) | copy-start | bytes 786436
  13.3 1.0 %copy-start.5 = (f32[2,512,256]{2,1,0:T(8,128)}, f32[2,512,256]{2,1,0:T(8,128)S(1)}, u32[]{:S(2)}) copy-start(f32[2,512,256]{2,1,0:T(8,128)S(1)} %get-tuple-element.29) | copy-start | bytes 3145732
  20.5 19.6 %collective-permute-start = (f32[2,512,256]{2,1,0:T(8,128)}, f32[2,512,256]{2,1,0:T(8,128)}, u32[]{:S(2)}, u32[]{:S(2)}) collective-permute-start(f32[2,512,256]{2,1,0:T(8,128)} %copy-done.5), channel_id=1, source_target_pairs={{0,1},{1,0},{2,3},{3,2},{4,5},{5,4},{6,7},{7,6},{8,9},{9,8},{10,11... | collective-permute-start | bytes 3145736 | tf_op jit(solution)/shard_map/ppermute | solution.py:265
  26.6 12.5 %all-to-all-start.1 = ((f32[8,44,256]{2,1,0:T(8,128)}), f32[8,44,256]{2,1,0:T(8,128)S(1)}, u32[]{:S(2)}, u32[]{:S(2)}) async-start(f32[8,44,256]{2,1,0:T(8,128)} %pack_plane.1), calls=%async_computation.1 | async-start | bytes 786432 | tf_op jit(solution)/shard_map/all_to_all | solution.py:270
  41.5 43.1 %copy-start.2 = (f32[256,256]{1,0:T(8,128)S(1)}, f32[256,256]{1,0:T(8,128)}, u32[]{:S(2)}) copy-start(f32[256,256]{1,0:T(8,128)} %l_inv.1) | copy-start | bytes 786436
  41.5 43.1 %copy-start.3 = (f32[256,256]{1,0:T(8,128)S(1)}, f32[256,256]{1,0:T(8,128)}, u32[]{:S(2)}) copy-start(f32[256,256]{1,0:T(8,128)} %u_inv.1) | copy-start | bytes 786436
  41.6 16.0 %collective-permute-start.1 = (f32[512,256]{1,0:T(8,128)S(1)}, f32[512,256]{1,0:T(8,128)S(1)}, u32[]{:S(2)}, u32[]{:S(2)}) collective-permute-start(f32[512,256]{1,0:T(8,128)S(1)} %get-tuple-element.32), channel_id=1, source_target_pairs={{0,2},{2,0},{1,3},{3,1},{4,6},{6,4},{5,7},{7,5},{8,10},{10,8},{9,1... | collective-permute-start | bytes 1572872 | tf_op jit(solution)/shard_map/ppermute | solution.py:284
  58.4 26.2 %all-to-all-start.3 = ((f32[8,32,512]{2,1,0:T(8,128)}), f32[8,32,512]{2,1,0:T(8,128)S(1)}, u32[]{:S(2)}, u32[]{:S(2)}) async-start(f32[8,32,512]{2,1,0:T(8,128)} %get-tuple-element.36), calls=%async_computation.3 | async-start | bytes 1048576 | tf_op jit(solution)/shard_map/all_to_all | solution.py:298

commit v3 on v2

--- a/solution.py
+++ b/solution.py
@@ -280,7 +280,6 @@
         compiler_params=params,
         name="plane_sum",
     )(place, got, panel_t, top_row)
-    send, slab_own, slab_give = lax.optimization_barrier((send, slab_own, slab_give))
     slab_got = lax.ppermute(slab_give, "xl", swap)
     got = lax.all_to_all(send, "y", 0, 0)
     got, slab_got = lax.optimization_barrier((got, slab_got))

time: 89.1 us -> 84.7 us (0.951)
  waiting for transfers between devices: 13.5 us -> 8.74 us
  starting transfers between devices: 30.5 us -> 31.6 us
    all_to_all x1, waiting for transfers between devices: 8.08 us -> 3.12 us  [shards(): got = lax.all_to_all(send, PLANE, 0, 0)]
    ppermute x1, starting transfers between devices: 2.32 us -> 3.43 us  [shards(): slab_got = lax.ppermute(slab_give, 'xl', swap)]
    all_gather x1, blocking collectives: 16.2 us -> 15.2 us  [shards(): rows_in = lax.all_gather(rows_out, PLANE)]
    all_to_all x1, blocking collectives: 13.6 us -> 14.6 us  [shards(): got = lax.all_to_all(send, 'y', 0, 0)]
  transfers between devices with their start and end apart: 5 -> 5, of which waited for: 2 -> 3; matrix products, arithmetic and copies ran while one was open for 0% -> 2% of each run, Pallas kernels for 5% -> 5%
where the time goes in v3:
time: 84.7 us; the launch traced here: 84.2 us
  starting transfers between devices  31.6 us (37%)
  blocking collectives  29.8 us (35%)
  Pallas kernels  11.4 us (13%)
  waiting for transfers between devices  8.74 us (10%)
  other arithmetic  1.49 us (2%)
  local copies, waits for them, and re-layouts  1.08 us (1%)
    all_gather x1, blocking collectives, shards(): rows_in = lax.all_gather(rows_out, PLANE)  15.2 us
    all_to_all x1, blocking collectives, shards(): got = lax.all_to_all(send, 'y', 0, 0)  14.6 us
    all_to_all x1, starting transfers between devices, shards(): panel_p = lax.all_to_all(panel_out, 'z', 0, 0)  10 us
    all_to_all x1, starting transfers between devices, shards(): top = lax.all_to_all(top, 'y', 0, 0)  7.65 us
    ppermute x1, starting transfers between devices, shards(): core_got = lax.ppermute(give, 'core', swap)  6.06 us
    all_to_all x1, waiting for transfers between devices, shards(): top = lax.all_to_all(top, 'y', 0, 0)  5.46 us
    all_to_all x1, starting transfers between devices, shards(): got = lax.all_to_all(send, PLANE, 0, 0)  4.42 us
    pallas_call x1, Pallas kernels, shards(): pl.pallas_call(pivot_kernel, out_shape=(jax.ShapeDtypeStruct((n_plane, bl...  3.61 us
  transfers between devices with their start and end apart: 5, of which 3 were waited for; matrix products, arithmetic and copies ran while one was open for 2% of the time, Pallas kernels for 5%

profile of v3, /device:TPU:1, one launch (start us, length us, event | category | flops | bytes accessed | tf_op | source)
XLA Modules:
  0.0 84.2 jit_solution(258080402253692228)
XLA Ops:
  0.0 0.0 copy-start
  0.0 0.0 copy-start.4
  0.0 1.9 %top_rows.1 = f32[8,40,256]{2,1,0:T(8,128)} custom-call(f32[2048,256]{1,0:T(8,128)} %bitcast.16, f32[32,2048]{1,0:T(8,128)} %panel.3), custom_call_target="tpu_custom_call" | custom-call | tf_op jit(solution)/shard_map/top_rows/pallas_call | solution.py:222
  1.9 0.1 pad_add_fusion.place
  2.0 7.7 %all-to-all-start = ((f32[8,40,256]{2,1,0:T(8,128)}), f32[8,40,256]{2,1,0:T(8,128)S(1)}, u32[]{:S(2)}, u32[]{:S(2)}) async-start(f32[8,40,256]{2,1,0:T(8,128)} %top_rows.1), calls=%async_computation | async-start | bytes 655360 | tf_op jit(solution)/shard_map/all_to_all | solution.py:232
  9.7 0.0 copy-done
  9.7 0.0 copy-done.4
  9.7 3.6 %pivot_rows.1 = (f32[8,32,256]{2,1,0:T(8,128)S(1)}, s32[1,512]{1,0:T(1,128)S(1)}, s32[512,128]{1,0:T(8,128)S(1)}, f32[2,512,256]{2,1,0:T(8,128)S(1)}) custom-call(s32[4]{0:T(128)S(1)} %pad_add_fusion.place, s32[1,256]{1,0:T(1,128)S(1)} %bitcast.20, f32[2048,256]{1,0:T(8,128)S(1)} %bitcast.17), custom_call_target="tpu_custom_call" | custom-call | flops 268435456 | bytes 8388608 | tf_op jit(solution)/shard_map/pivot_rows/pallas_call | solution.py:234
  13.3 0.0 copy-start.5
  13.3 1.0 %copy-done.5 = f32[2,512,256]{2,1,0:T(8,128)} copy-done((f32[2,512,256]{2,1,0:T(8,128)}, f32[2,512,256]{2,1,0:T(8,128)S(1)}, u32[]{:S(2)}) %copy-start.5) | copy-done | bytes 1048600
  14.3 5.5 %all-to-all-done.got = f32[8,40,256]{2,1,0:T(8,128)S(1)} async-done(((f32[8,40,256]{2,1,0:T(8,128)}), f32[8,40,256]{2,1,0:T(8,128)S(1)}, u32[]{:S(2)}, u32[]{:S(2)}) %all-to-all-start) | async-done | bytes 327712 | tf_op jit(solution)/shard_map/all_to_all | solution.py:232
  19.8 0.8 pack_plane.1
  20.5 6.1 %collective-permute-start = (f32[2,512,256]{2,1,0:T(8,128)}, f32[2,512,256]{2,1,0:T(8,128)}, u32[]{:S(2)}, u32[]{:S(2)}) collective-permute-start(f32[2,512,256]{2,1,0:T(8,128)} %copy-done.5), channel_id=1, source_target_pairs={{0,1},{1,0},{2,3},{3,2},{4,5},{5,4},{6,7},{7,6},{8,9},{9,8},{10,11... | collective-permute-start | bytes 3145736 | tf_op jit(solution)/shard_map/ppermute | solution.py:265
  26.6 4.4 %all-to-all-start.1 = ((f32[8,44,256]{2,1,0:T(8,128)}), f32[8,44,256]{2,1,0:T(8,128)S(1)}, u32[]{:S(2)}, u32[]{:S(2)}) async-start(f32[8,44,256]{2,1,0:T(8,128)} %pack_plane.1), calls=%async_computation.1 | async-start | bytes 786432 | tf_op jit(solution)/shard_map/all_to_all | solution.py:270
  31.0 0.0 collective-permute-done
  31.0 1.4 %bitcast_add_fusion = f32[2,512,256]{2,1,0:T(8,128)S(1)} fusion(f32[2,512,256]{2,1,0:T(8,128)} %collective-permute-done, f32[2,2,512,256]{3,2,1,0:T(8,128)S(1)} %bitcast.18, s32[]{:T(128)S(6)} %select_n.11), kind=kLoop, calls=%fused_computation | loop fusion | flops 262144 | bytes 3145732 | tf_op jit(solution)/shard_map/add | solution.py:267
  32.4 0.1 dynamic-slice_bitcast_fusion
  32.5 0.0 copy-start.2
  32.5 0.0 copy-start.3
  32.6 3.4 %collective-permute-start.1 = (f32[512,256]{1,0:T(8,128)S(1)}, f32[512,256]{1,0:T(8,128)S(1)}, u32[]{:S(2)}, u32[]{:S(2)}) collective-permute-start(f32[512,256]{1,0:T(8,128)S(1)} %get-tuple-element.33), channel_id=1, source_target_pairs={{0,2},{2,0},{1,3},{3,1},{4,6},{6,4},{5,7},{7,5},{8,10},{10,8},{9,1... | collective-permute-start | bytes 1572872 | tf_op jit(solution)/shard_map/ppermute | solution.py:283
  36.0 3.1 %all-to-all-done.1.got = f32[8,44,256]{2,1,0:T(8,128)S(1)} async-done(((f32[8,44,256]{2,1,0:T(8,128)}), f32[8,44,256]{2,1,0:T(8,128)S(1)}, u32[]{:S(2)}, u32[]{:S(2)}) %all-to-all-start.1) | async-done | bytes 360480 | tf_op jit(solution)/shard_map/all_to_all | solution.py:270
  39.1 0.0 copy-done.1
  39.1 1.0 %plane_sum.1 = (f32[8,36,256]{2,1,0:T(8,128)S(1)}, f32[32,512]{1,0:T(8,128)S(1)}) custom-call(s32[4]{0:T(128)S(1)} %pad_add_fusion.place, f32[8,44,256]{2,1,0:T(8,128)S(1)} %all-to-all-done.1.got, f32[32,2048]{1,0:T(8,128)S(1)} %copy-done.1, s32[1,512]{1,0:T(1,128)S(1)} %get-tuple-element.25.top_row), custom_call_target="tpu_custom_call" | custom-call | tf_op jit(solution)/shard_map/plane_sum/pallas_call | solution.py:271
  40.1 14.6 %all_to_all.20.got = f32[8,36,256]{2,1,0:T(8,128)S(1)} all-to-all(f32[8,36,256]{2,1,0:T(8,128)S(1)} %get-tuple-element.26), channel_id=1, replica_groups=mesh['y'=8,'xh'=2,'z'=8,'xl'=2,'core'=2] {'y'}, dimensions={0} | all-to-all | bytes 589824 | tf_op jit(solution)/shard_map/all_to_all | solution.py:284
  54.7 0.0 collective-permute-done.1.slab_got
  54.7 0.8 column_sum.1
  55.6 10.0 %all-to-all-start.3 = ((f32[8,32,512]{2,1,0:T(8,128)}), f32[8,32,512]{2,1,0:T(8,128)S(1)}, u32[]{:S(2)}, u32[]{:S(2)}) async-start(f32[8,32,512]{2,1,0:T(8,128)} %get-tuple-element.30), calls=%async_computation.3 | async-start | bytes 1048576 | tf_op jit(solution)/shard_map/all_to_all | solution.py:297
  65.6 15.2 %all-gather = f32[512,256]{1,0:T(8,128)S(1)} all-gather(f32[64,256]{1,0:T(8,128)S(1)} %get-tuple-element.31), channel_id=2, replica_groups=mesh['y'=8,'xh'=2,'z'=8,'xl'=2,'core'=2] {'xh','xl','core'}, dimensions={0}, use_global_device_ids=true | all-gather | bytes 589824 | tf_op jit(solution)/shard_map/all_gather | solution.py:298
  80.8 0.2 all-to-all-done.3.panel
  81.0 0.0 copy-done.2
  81.0 0.0 copy-done.3
  81.0 3.2 %update_rows.1 = f32[512,256]{1,0:T(8,128)} custom-call(s32[4]{0:T(128)S(1)} %pad_add_fusion.place, f32[512,256]{1,0:T(8,128)S(1)} %get-tuple-element.34.slab, f32[512,256]{1,0:T(8,128)S(1)} %collective-permute-done.1.slab_got, f32[8,32,512]{2,1,0:T(8,128)S(1)} %all-to-all-done.3.panel, f32[8,64,256]{2,1,0:T(8,128)S(1)} %bitcast.19, ...), custom_call_target="tpu_custom_call" | custom-call | tf_op jit(solution)/shard_map/update_rows/pallas_call | solution.py:299
  (1 shorter events, 0.0 us)
Async XLA Ops:
  0.0 9.7 %copy-start = (f32[1,2048,256]{2,1,0:T(8,128)S(1)}, f32[1,2048,256]{2,1,0:T(8,128)}, u32[]{:S(2)}) copy-start(f32[1,2048,256]{2,1,0:T(8,128)} %param.5) | copy-start | bytes 6291460
  0.0 9.7 %copy-start.4 = (s32[256]{0:T(256)S(1)}, s32[256]{0:T(256)}, u32[]{:S(2)}) copy-start(s32[256]{0:T(256)} %param.9) | copy-start | bytes 3076
  2.0 17.7 %all-to-all-start = ((f32[8,40,256]{2,1,0:T(8,128)}), f32[8,40,256]{2,1,0:T(8,128)S(1)}, u32[]{:S(2)}, u32[]{:S(2)}) async-start(f32[8,40,256]{2,1,0:T(8,128)} %top_rows.1), calls=%async_computation | async-start | bytes 655360 | tf_op jit(solution)/shard_map/all_to_all | solution.py:232
  13.3 1.0 %copy-start.5 = (f32[2,512,256]{2,1,0:T(8,128)}, f32[2,512,256]{2,1,0:T(8,128)S(1)}, u32[]{:S(2)}) copy-start(f32[2,512,256]{2,1,0:T(8,128)S(1)} %get-tuple-element.23) | copy-start | bytes 3145732
  20.5 10.5 %collective-permute-start = (f32[2,512,256]{2,1,0:T(8,128)}, f32[2,512,256]{2,1,0:T(8,128)}, u32[]{:S(2)}, u32[]{:S(2)}) collective-permute-start(f32[2,512,256]{2,1,0:T(8,128)} %copy-done.5), channel_id=1, source_target_pairs={{0,1},{1,0},{2,3},{3,2},{4,5},{5,4},{6,7},{7,6},{8,9},{9,8},{10,11... | collective-permute-start | bytes 3145736 | tf_op jit(solution)/shard_map/ppermute | solution.py:265
  26.6 12.5 %all-to-all-start.1 = ((f32[8,44,256]{2,1,0:T(8,128)}), f32[8,44,256]{2,1,0:T(8,128)S(1)}, u32[]{:S(2)}, u32[]{:S(2)}) async-start(f32[8,44,256]{2,1,0:T(8,128)} %pack_plane.1), calls=%async_computation.1 | async-start | bytes 786432 | tf_op jit(solution)/shard_map/all_to_all | solution.py:270
  31.0 8.1 %copy-start.1 = (f32[32,2048]{1,0:T(8,128)S(1)}, f32[32,2048]{1,0:T(8,128)}, u32[]{:S(2)}) copy-start(f32[32,2048]{1,0:T(8,128)} %panel.3) | copy-start | bytes 786436
  32.5 48.4 %copy-start.2 = (f32[256,256]{1,0:T(8,128)S(1)}, f32[256,256]{1,0:T(8,128)}, u32[]{:S(2)}) copy-start(f32[256,256]{1,0:T(8,128)} %l_inv.1) | copy-start | bytes 786436
  32.5 48.4 %copy-start.3 = (f32[256,256]{1,0:T(8,128)S(1)}, f32[256,256]{1,0:T(8,128)}, u32[]{:S(2)}) copy-start(f32[256,256]{1,0:T(8,128)} %u_inv.1) | copy-start | bytes 786436
  32.6 22.2 %collective-permute-start.1 = (f32[512,256]{1,0:T(8,128)S(1)}, f32[512,256]{1,0:T(8,128)S(1)}, u32[]{:S(2)}, u32[]{:S(2)}) collective-permute-start(f32[512,256]{1,0:T(8,128)S(1)} %get-tuple-element.33), channel_id=1, source_target_pairs={{0,2},{2,0},{1,3},{3,1},{4,6},{6,4},{5,7},{7,5},{8,10},{10,8},{9,1... | collective-permute-start | bytes 1572872 | tf_op jit(solution)/shard_map/ppermute | solution.py:283
  55.6 25.4 %all-to-all-start.3 = ((f32[8,32,512]{2,1,0:T(8,128)}), f32[8,32,512]{2,1,0:T(8,128)S(1)}, u32[]{:S(2)}, u32[]{:S(2)}) async-start(f32[8,32,512]{2,1,0:T(8,128)} %get-tuple-element.30), calls=%async_computation.3 | async-start | bytes 1048576 | tf_op jit(solution)/shard_map/all_to_all | solution.py:297

commit v4 on v3

--- a/solution.py
+++ b/solution.py
@@ -51,7 +51,7 @@
         copy.wait()
 
 
-def pivot_kernel(place, pivots, slab, send, top_row, top_col, give, source_v, source_s, sem):
+def pivot_kernel(place, pivots, slab, send, top_row, top_col, first, second, source_v, source_s, sem):
     rows, columns = slab.shape
     width = pivots.shape[1]
     groups, block, _ = send.shape
@@ -98,24 +98,30 @@
     )
     own_along = share_start + lax.broadcasted_iota(I32, (width, share), 1)
     top_row[...] = jnp.max(jnp.where(target_col == own_along, content_col, -1), axis=0, keepdims=True)
-    own_down = share_start + lax.broadcasted_iota(I32, (share, width), 0)
-    found = jnp.max(jnp.where(target_row == own_down, content_row, -1), axis=1, keepdims=True)
-    top_col[...] = jnp.broadcast_to(found, top_col.shape)
-    for half in range(give.shape[0]):
+    square = lax.broadcasted_iota(I32, (128, 128), 0) == lax.broadcasted_iota(I32, (128, 128), 1)
+    for start in range(0, share, 128):
+        piece = jnp.broadcast_to(top_row[:, start : start + 128], (128, 128))
+        found = jnp.max(jnp.where(square, piece, -1), axis=1, keepdims=True)
+        top_col[start : start + 128, :] = jnp.broadcast_to(found, (128, 128))
+    local_row = source[:1] - row_start
+    owned_row = jnp.where((local_row >= 0) & (local_row < rows), 1.0, 0.0).astype(F32)
+    owned_all = jnp.broadcast_to(owned_row, (width, width))
+    owned = jnp.max(jnp.where(along == down, owned_all, 0.0), axis=1, keepdims=True)
+    for half, give in enumerate((first, second)):
         start = pl.multiple_of((2 * half + place[3]) * share, share)
-        give[half] = slab[pl.ds(start, share), :]
+        give[...] = slab[pl.ds(start, share), :]
     to_scalar.wait()
 
     def gather(group, carry):
         for slot in range(block):
-            local = source_s[0, group * block + slot] - row_start
-            owned = (local >= 0) & (local < rows)
-            at = jnp.where(owned, local, 0)
-            keep = jnp.where(owned, 1.0, 0.0).astype(F32)
-            send[group, slot : slot + 1, :] = slab[pl.ds(at, 1), :] * keep
+            at = jnp.clip(source_s[0, group * block + slot] - row_start, 0, rows - 1)
+            send[group, slot : slot + 1, :] = slab[pl.ds(at, 1), :]
         return carry
 
     lax.fori_loop(0, groups, gather, 0)
+    for group in range(groups):
+        keep = owned[group * block : (group + 1) * block] > 0.0
+        send[group] = jnp.where(keep, send[group], 0.0)
 
 
 def pack_kernel(moved, got, send):
@@ -129,21 +135,25 @@
         send[target, block + fill :, :] = got[0, target * part : (target + 1) * part, :]
 
 
-def plane_sum_kernel(place, got, panel, top_row, send, panel_out, top_panel, *, block):
+def plane_sum_kernel(got, send, *, block):
     groups = got.shape[0]
-    first = groups // 2
     part = send.shape[1] - block
-    fill = got.shape[1] - block - part
+    both = got.shape[1]
     moved = got[0, :block, :]
     for source in range(1, groups):
         moved = moved + got[source, :block, :]
-    top = got[0, block + fill :, :]
-    for source in range(1, first):
-        top = top + got[source, block + fill :, :]
+    top = got[0, both - part :, :]
+    for source in range(1, groups // 2):
+        top = top + got[source, both - part :, :]
     for target in range(send.shape[0]):
         send[target, :block, :] = moved
         send[target, block:, :] = top
-    for source in range(first):
+
+
+def panel_kernel(place, got, panel, top_row, panel_out, top_panel, *, block):
+    layers = got.shape[0] // 2
+    fill = panel.shape[0] // layers
+    for source in range(layers):
         top_panel[source * fill : (source + 1) * fill, :] = got[source, block : block + fill, :]
     share = top_row.shape[1]
     width = top_panel.shape[1]
@@ -152,10 +162,12 @@
     chosen = jnp.where(slot == lands, 1.0, 0.0).astype(F32)
     replaced = jnp.dot(top_panel[...], chosen, precision=HIGHEST, preferred_element_type=F32)
     own = panel[:, pl.ds(pl.multiple_of(place[2] * share, share), share)]
-    panel_out[...] = jnp.where(lands >= 0, replaced, own)
-
-
-def column_kernel(got, panel, rows_out, panel_out):
+    fixed = jnp.where(lands >= 0, replaced, own)
+    for target in range(panel_out.shape[0]):
+        panel_out[target] = fixed
+
+
+def column_kernel(got, rows_out):
     groups, both, _ = got.shape
     block = rows_out.shape[0] // 2
     part = both - block
@@ -165,8 +177,6 @@
     rows_out[:block, :] = moved
     for source in range(groups):
         rows_out[block + source * part : block + (source + 1) * part, :] = got[source, block:, :]
-    for target in range(panel_out.shape[0]):
-        panel_out[target] = panel[...]
 
 
 def update_kernel(place, slab, slab_got, panel, rows_in, l_inv, u_inv, top_col, out, *, n_y):
@@ -231,16 +241,17 @@
     top, place = lax.optimization_barrier((top, place))
     top = lax.all_to_all(top, "y", 0, 0)
 
-    moved, top_row, top_col, give = pl.pallas_call(
+    moved, top_row, top_col, first, second = pl.pallas_call(
         pivot_kernel,
         out_shape=(
             jax.ShapeDtypeStruct((n_plane, block, columns), F32),
             jax.ShapeDtypeStruct((1, share), I32),
             jax.ShapeDtypeStruct((share, 128), I32),
-            jax.ShapeDtypeStruct((n_depth // 2, share, columns), F32),
+            jax.ShapeDtypeStruct((share, columns), F32),
+            jax.ShapeDtypeStruct((share, columns), F32),
         ),
         in_specs=[SMEM, VMEM, VMEM],
-        out_specs=(VMEM, VMEM, VMEM, VMEM),
+        out_specs=(VMEM,) * 5,
         scratch_shapes=[
             pltpu.VMEM((8, width), I32),
             pltpu.SMEM((8, width), I32),
@@ -261,40 +272,45 @@
         compiler_params=params,
         name="pack_plane",
     )(moved, top)
-    send, give = lax.optimization_barrier((send, give))
-    core_got = lax.ppermute(give, "core", swap)
-    by_core = slab_local.reshape(n_depth // 2, 2, share, columns)
-    half = lax.dynamic_index_in_dim(by_core, core, 1, keepdims=False) + core_got
-    slab_own = lax.dynamic_index_in_dim(half, x_index, 0, keepdims=False)
-    slab_give = lax.dynamic_index_in_dim(half, 1 - x_index, 0, keepdims=False)
+    first_got = lax.ppermute(first, "core", swap)
+    second_got = lax.ppermute(second, "core", swap)
+    near = lax.dynamic_slice_in_dim(slab_local, (2 * x_index + core) * share, share)
+    far = lax.dynamic_slice_in_dim(slab_local, (2 * (1 - x_index) + core) * share, share)
+    slab_own = near + jnp.where(x_index == 0, first_got, second_got)
+    slab_give = far + jnp.where(x_index == 0, second_got, first_got)
     got = lax.all_to_all(send, PLANE, 0, 0)
-    send, panel_own = pl.pallas_call(
+    send = pl.pallas_call(
         functools.partial(plane_sum_kernel, block=block),
-        out_shape=(
-            jax.ShapeDtypeStruct((n_y, block + part, columns), F32),
-            jax.ShapeDtypeStruct((tall, share), F32),
+        out_shape=jax.ShapeDtypeStruct((n_y, block + part, columns), F32),
+        in_specs=[VMEM],
+        out_specs=VMEM,
+        compiler_params=params,
+        name="plane_sum",
+    )(got)
+    panel_out = pl.pallas_call(
+        functools.partial(panel_kernel, block=block),
+        out_shape=jax.ShapeDtypeStruct((n_z, tall, share), F32),
+        in_specs=[SMEM, VMEM, VMEM, VMEM],
+        out_specs=VMEM,
+        scratch_shapes=[pltpu.VMEM((tall, width), F32)],
+        compiler_params=params,
+        cost_estimate=pl.CostEstimate(
+            flops=2 * rows * width * columns, bytes_accessed=8 * rows * columns, transcendentals=0
         ),
-        in_specs=[SMEM, VMEM, VMEM, VMEM],
-        out_specs=(VMEM, VMEM),
-        scratch_shapes=[pltpu.VMEM((tall, width), F32)],
-        compiler_params=params,
-        name="plane_sum",
+        name="panel_columns",
     )(place, got, panel_t, top_row)
     slab_got = lax.ppermute(slab_give, "xl", swap)
     got = lax.all_to_all(send, "y", 0, 0)
-    got, slab_got = lax.optimization_barrier((got, slab_got))
-    rows_out, panel_out = pl.pallas_call(
+    got, panel_out, slab_got = lax.optimization_barrier((got, panel_out, slab_got))
+    panel_p = lax.all_to_all(panel_out, "z", 0, 0)
+    rows_out = pl.pallas_call(
         column_kernel,
-        out_shape=(
-            jax.ShapeDtypeStruct((2 * block, columns), F32),
-            jax.ShapeDtypeStruct((n_z, tall, share), F32),
-        ),
-        in_specs=[VMEM, VMEM],
-        out_specs=(VMEM, VMEM),
+        out_shape=jax.ShapeDtypeStruct((2 * block, columns), F32),
+        in_specs=[VMEM],
+        out_specs=VMEM,
         compiler_params=params,
         name="column_sum",
-    )(got, panel_own)
-    panel_p = lax.all_to_all(panel_out, "z", 0, 0)
+    )(got)
     rows_in = lax.all_gather(rows_out, PLANE)
     return pl.pallas_call(
         functools.partial(update_kernel, n_y=n_y),

time: 84.7 us -> 83.6 us (0.987); the launches traced: 84.2 us -> 82 us
  blocking collectives: 29.8 us -> 15.3 us
  starting transfers between devices: 31.6 us -> 38.8 us
  waiting for transfers between devices: 8.74 us -> 12.8 us
  Pallas kernels: 11.4 us -> 12.8 us
  local copies, waits for them, and re-layouts: 1.08 us -> 0.02 us
    all_to_all x1 -> x0, blocking collectives: 14.6 us -> none  [shards(): got = lax.all_to_all(send, 'y', 0, 0)]
    all_to_all x0 -> x1, waiting for transfers between devices: none -> 6.42 us  [shards(): got = lax.all_to_all(send, 'y', 0, 0)]
    all_to_all x1, waiting for transfers between devices: 5.46 us -> 0.01 us  [shards(): top = lax.all_to_all(top, 'y', 0, 0)]
    ppermute x1, waiting for transfers between devices: 0.01 us -> 3.73 us  [shards(): slab_got = lax.ppermute(slab_give, 'xl', swap)]
    all_to_all x0 -> x1, starting transfers between devices: none -> 3.56 us  [shards(): got = lax.all_to_all(send, 'y', 0, 0)]
    all_to_all x1, starting transfers between devices: 4.42 us -> 7.58 us  [shards(): got = lax.all_to_all(send, PLANE, 0, 0)]
    unnamed x12 -> x10, local copies, waits for them, and re-layouts: 1 us -> 0.02 us
    pallas_call x1 -> x2, Pallas kernels: 0.84 us -> 1.81 us  [the longest x1 1.79 us: shards(): pl.pallas_call(functools.partial(panel_kernel, block=block), out_shape=ja...]
  transfers between devices with their start and end apart: 5 -> 7, of which waited for: 3 -> 3; matrix products, arithmetic and copies ran while one was open for 2% -> 3% of each run, Pallas kernels for 5% -> 9%
where the time goes in v4:
time: 83.6 us; the launch traced here: 82 us
  starting transfers between devices  38.8 us (46%)
  blocking collectives  15.3 us (18%)
  Pallas kernels  12.8 us (15%)
  waiting for transfers between devices  12.8 us (15%)
  other arithmetic  2.26 us (3%)
    all_gather x1, blocking collectives, shards(): rows_in = lax.all_gather(rows_out, PLANE)  15.3 us
    all_to_all x1, starting transfers between devices, shards(): panel_p = lax.all_to_all(panel_out, 'z', 0, 0)  10.2 us
    all_to_all x1, starting transfers between devices, shards(): top = lax.all_to_all(top, 'y', 0, 0)  7.65 us
    all_to_all x1, starting transfers between devices, shards(): got = lax.all_to_all(send, PLANE, 0, 0)  7.58 us
    all_to_all x1, waiting for transfers between devices, shards(): got = lax.all_to_all(send, 'y', 0, 0)  6.42 us
    ppermute x1, starting transfers between devices, shards(): second_got = lax.ppermute(second, 'core', swap)  4.58 us
    pallas_call x1, Pallas kernels, shards(): pl.pallas_call(pivot_kernel, out_shape=(jax.ShapeDtypeStruct((n_plane, bl...  4.4 us
    ppermute x1, waiting for transfers between devices, shards(): slab_got = lax.ppermute(slab_give, 'xl', swap)  3.73 us
  transfers between devices with their start and end apart: 7, of which 3 were waited for; matrix products, arithmetic and copies ran while one was open for 3% of the time, Pallas kernels for 9%

profile of v4, /device:TPU:1, one launch (start us, length us, event | category | flops | bytes accessed | tf_op | source)
XLA Modules:
  0.0 82.0 jit_solution(2019166502990256416)
XLA Ops:
  0.0 0.0 copy-start
  0.0 0.0 copy-start.4
  0.0 1.9 %top_rows.1 = f32[8,40,256]{2,1,0:T(8,128)} custom-call(f32[2048,256]{1,0:T(8,128)} %bitcast.11, f32[32,2048]{1,0:T(8,128)} %panel.3), custom_call_target="tpu_custom_call" | custom-call | tf_op jit(solution)/shard_map/top_rows/pallas_call | solution.py:232
  2.0 0.1 pad_add_fusion.place
  2.0 7.7 %all-to-all-start = ((f32[8,40,256]{2,1,0:T(8,128)}), f32[8,40,256]{2,1,0:T(8,128)S(1)}, u32[]{:S(2)}, u32[]{:S(2)}) async-start(f32[8,40,256]{2,1,0:T(8,128)} %top_rows.1), calls=%async_computation | async-start | bytes 655360 | tf_op jit(solution)/shard_map/all_to_all | solution.py:242
  9.7 0.0 copy-done
  9.7 0.0 copy-done.4
  9.7 4.4 %pivot_rows.1 = (f32[8,32,256]{2,1,0:T(8,128)S(1)}, s32[1,512]{1,0:T(1,128)S(1)}, s32[512,128]{1,0:T(8,128)S(1)}, f32[512,256]{1,0:T(8,128)}, f32[512,256]{1,0:T(8,128)}) custom-call(s32[4]{0:T(128)S(1)} %pad_add_fusion.place, s32[1,256]{1,0:T(1,128)S(1)} %bitcast.14, f32[2048,256]{1,0:T(8,128)S(1)} %bitcast.12), custom_call_target="tpu_custom_call" | custom-call | flops 268435456 | bytes 8388608 | tf_op jit(solution)/shard_map/pivot_rows/pallas_call | solution.py:244
  14.1 4.6 %collective-permute-start.1 = (f32[512,256]{1,0:T(8,128)}, f32[512,256]{1,0:T(8,128)}, u32[]{:S(2)}, u32[]{:S(2)}) collective-permute-start(f32[512,256]{1,0:T(8,128)} %get-tuple-element.17), channel_id=1, source_target_pairs={{0,1},{1,0},{2,3},{3,2},{4,5},{5,4},{6,7},{7,6},{8,9},{9,8},{10,11... | collective-permute-start | bytes 1572872 | tf_op jit(solution)/shard_map/ppermute | solution.py:276
  18.7 1.9 %collective-permute-start = (f32[512,256]{1,0:T(8,128)}, f32[512,256]{1,0:T(8,128)}, u32[]{:S(2)}, u32[]{:S(2)}) collective-permute-start(f32[512,256]{1,0:T(8,128)} %get-tuple-element.16), channel_id=1, source_target_pairs={{0,1},{1,0},{2,3},{3,2},{4,5},{5,4},{6,7},{7,6},{8,9},{9,8},{10,11... | collective-permute-start | bytes 1572872 | tf_op jit(solution)/shard_map/ppermute | solution.py:275
  20.6 0.0 all-to-all-done.got
  20.6 0.8 pack_plane.1
  21.4 7.6 %all-to-all-start.1 = ((f32[8,44,256]{2,1,0:T(8,128)}), f32[8,44,256]{2,1,0:T(8,128)S(1)}, u32[]{:S(2)}, u32[]{:S(2)}) async-start(f32[8,44,256]{2,1,0:T(8,128)} %pack_plane.1), calls=%async_computation.1 | async-start | bytes 786432 | tf_op jit(solution)/shard_map/all_to_all | solution.py:281
  29.0 0.0 copy-start.1
  29.0 0.0 collective-permute-done.1
  29.0 0.0 collective-permute-done
  29.0 2.2 %bitcast_add_fusion = (f32[512,256]{1,0:T(8,128)}, f32[512,256]{1,0:T(8,128)S(1)}) fusion(f32[512,256]{1,0:T(8,128)} %collective-permute-done.1, f32[512,256]{1,0:T(8,128)} %collective-permute-done, f32[1,2048,256]{2,1,0:T(8,128)S(1)} %copy-done, s32[]{:T(128)S(6)} %select_n.21, pred[]{:T(512)S(6)} %eq.4, s32[]{:T(128)S(6)} %select_n.18), kind=kLoop, calls=%fused_computation | loop fusion | flops 524288 | bytes 3145737 | tf_op jit(solution)/shard_map/add | solution.py:280
  31.2 3.3 %collective-permute-start.2 = (f32[512,256]{1,0:T(8,128)}, f32[512,256]{1,0:T(8,128)S(1)}, u32[]{:S(2)}, u32[]{:S(2)}) collective-permute-start(f32[512,256]{1,0:T(8,128)} %get-tuple-element.25), channel_id=1, source_target_pairs={{0,2},{2,0},{1,3},{3,1},{4,6},{6,4},{5,7},{7,5},{8,10},{10,8},{9,1... | collective-permute-start | bytes 1572872 | tf_op jit(solution)/shard_map/ppermute | solution.py:302
  34.5 2.6 %all-to-all-done.1.got = f32[8,44,256]{2,1,0:T(8,128)S(1)} async-done(((f32[8,44,256]{2,1,0:T(8,128)}), f32[8,44,256]{2,1,0:T(8,128)S(1)}, u32[]{:S(2)}, u32[]{:S(2)}) %all-to-all-start.1) | async-done | bytes 360480 | tf_op jit(solution)/shard_map/all_to_all | solution.py:281
  37.1 0.8 plane_sum.1
  37.8 0.0 copy-start.2
  37.8 3.6 %all-to-all-start.2 = ((f32[8,36,256]{2,1,0:T(8,128)}), f32[8,36,256]{2,1,0:T(8,128)S(1)}, u32[]{:S(2)}, u32[]{:S(2)}) async-start(f32[8,36,256]{2,1,0:T(8,128)} %plane_sum.1), calls=%async_computation.2 | async-start | bytes 655360 | tf_op jit(solution)/shard_map/all_to_all | solution.py:303
  41.4 0.0 copy-done.1
  41.4 1.8 %panel_columns.1 = f32[8,32,512]{2,1,0:T(8,128)} custom-call(s32[4]{0:T(128)S(1)} %pad_add_fusion.place, f32[8,44,256]{2,1,0:T(8,128)S(1)} %all-to-all-done.1.got, f32[32,2048]{1,0:T(8,128)S(1)} %copy-done.1, s32[1,512]{1,0:T(1,128)S(1)} %get-tuple-element.20.top_row), custom_call_target="tpu_custom_call" | custom-call | flops 268435456 | bytes 4194304 | tf_op jit(solution)/shard_map/panel_columns/pallas_call | solution.py:290
  43.2 3.7 %collective-permute-done.2.slab_got = f32[512,256]{1,0:T(8,128)S(1)} collective-permute-done((f32[512,256]{1,0:T(8,128)}, f32[512,256]{1,0:T(8,128)S(1)}, u32[]{:S(2)}, u32[]{:S(2)}) %collective-permute-start.2) | collective-permute-done | bytes 524320 | tf_op jit(solution)/shard_map/ppermute | solution.py:302
  46.9 6.4 %all-to-all-done.2.got = f32[8,36,256]{2,1,0:T(8,128)S(1)} async-done(((f32[8,36,256]{2,1,0:T(8,128)}), f32[8,36,256]{2,1,0:T(8,128)S(1)}, u32[]{:S(2)}, u32[]{:S(2)}) %all-to-all-start.2) | async-done | bytes 294944 | tf_op jit(solution)/shard_map/all_to_all | solution.py:303
  53.4 10.2 %all-to-all-start.3 = ((f32[8,32,512]{2,1,0:T(8,128)}), f32[8,32,512]{2,1,0:T(8,128)S(1)}, u32[]{:S(2)}, u32[]{:S(2)}) async-start(f32[8,32,512]{2,1,0:T(8,128)} %panel_columns.1), calls=%async_computation.3 | async-start | bytes 1048576 | tf_op jit(solution)/shard_map/all_to_all | solution.py:305
  63.6 15.3 %all-gather = f32[512,256]{1,0:T(8,128)S(1)} all-gather(f32[64,256]{1,0:T(8,128)S(1)} %column_sum.1), channel_id=2, replica_groups=mesh['y'=8,'xh'=2,'z'=8,'xl'=2,'core'=2] {'xh','xl','core'}, dimensions={0}, use_global_device_ids=true | all-gather | bytes 589824 | tf_op jit(solution)/shard_map/all_gather | solution.py:314
  78.8 0.0 all-to-all-done.3.panel
  78.8 0.0 copy-done.2
  78.8 0.0 copy-done.3
  78.8 3.2 %update_rows.1 = f32[512,256]{1,0:T(8,128)} custom-call(s32[4]{0:T(128)S(1)} %pad_add_fusion.place, f32[512,256]{1,0:T(8,128)S(1)} %get-tuple-element.26.slab, f32[512,256]{1,0:T(8,128)S(1)} %collective-permute-done.2.slab_got, f32[8,32,512]{2,1,0:T(8,128)S(1)} %all-to-all-done.3.panel, f32[8,64,256]{2,1,0:T(8,128)S(1)} %bitcast.13, ...), custom_call_target="tpu_custom_call" | custom-call | tf_op jit(solution)/shard_map/update_rows/pallas_call | solution.py:315
  (2 shorter events, 0.0 us)
Async XLA Ops:
  0.0 9.7 %copy-start = (f32[1,2048,256]{2,1,0:T(8,128)S(1)}, f32[1,2048,256]{2,1,0:T(8,128)}, u32[]{:S(2)}) copy-start(f32[1,2048,256]{2,1,0:T(8,128)} %param.5) | copy-start | bytes 6291460
  0.0 9.7 %copy-start.4 = (s32[256]{0:T(256)S(1)}, s32[256]{0:T(256)}, u32[]{:S(2)}) copy-start(s32[256]{0:T(256)} %param.9) | copy-start | bytes 3076
  2.0 18.6 %all-to-all-start = ((f32[8,40,256]{2,1,0:T(8,128)}), f32[8,40,256]{2,1,0:T(8,128)S(1)}, u32[]{:S(2)}, u32[]{:S(2)}) async-start(f32[8,40,256]{2,1,0:T(8,128)} %top_rows.1), calls=%async_computation | async-start | bytes 655360 | tf_op jit(solution)/shard_map/all_to_all | solution.py:242
  14.1 14.9 %collective-permute-start.1 = (f32[512,256]{1,0:T(8,128)}, f32[512,256]{1,0:T(8,128)}, u32[]{:S(2)}, u32[]{:S(2)}) collective-permute-start(f32[512,256]{1,0:T(8,128)} %get-tuple-element.17), channel_id=1, source_target_pairs={{0,1},{1,0},{2,3},{3,2},{4,5},{5,4},{6,7},{7,6},{8,9},{9,8},{10,11... | collective-permute-start | bytes 1572872 | tf_op jit(solution)/shard_map/ppermute | solution.py:276
  18.7 10.3 %collective-permute-start = (f32[512,256]{1,0:T(8,128)}, f32[512,256]{1,0:T(8,128)}, u32[]{:S(2)}, u32[]{:S(2)}) collective-permute-start(f32[512,256]{1,0:T(8,128)} %get-tuple-element.16), channel_id=1, source_target_pairs={{0,1},{1,0},{2,3},{3,2},{4,5},{5,4},{6,7},{7,6},{8,9},{9,8},{10,11... | collective-permute-start | bytes 1572872 | tf_op jit(solution)/shard_map/ppermute | solution.py:275
  21.4 15.7 %all-to-all-start.1 = ((f32[8,44,256]{2,1,0:T(8,128)}), f32[8,44,256]{2,1,0:T(8,128)S(1)}, u32[]{:S(2)}, u32[]{:S(2)}) async-start(f32[8,44,256]{2,1,0:T(8,128)} %pack_plane.1), calls=%async_computation.1 | async-start | bytes 786432 | tf_op jit(solution)/shard_map/all_to_all | solution.py:281
  29.0 12.4 %copy-start.1 = (f32[32,2048]{1,0:T(8,128)S(1)}, f32[32,2048]{1,0:T(8,128)}, u32[]{:S(2)}) copy-start(f32[32,2048]{1,0:T(8,128)} %panel.3) | copy-start | bytes 786436
  31.2 15.7 %collective-permute-start.2 = (f32[512,256]{1,0:T(8,128)}, f32[512,256]{1,0:T(8,128)S(1)}, u32[]{:S(2)}, u32[]{:S(2)}) collective-permute-start(f32[512,256]{1,0:T(8,128)} %get-tuple-element.25), channel_id=1, source_target_pairs={{0,2},{2,0},{1,3},{3,1},{4,6},{6,4},{5,7},{7,5},{8,10},{10,8},{9,1... | collective-permute-start | bytes 1572872 | tf_op jit(solution)/shard_map/ppermute | solution.py:302
  37.8 41.0 %copy-start.2 = (f32[256,256]{1,0:T(8,128)S(1)}, f32[256,256]{1,0:T(8,128)}, u32[]{:S(2)}) copy-start(f32[256,256]{1,0:T(8,128)} %l_inv.1) | copy-start | bytes 786436
  37.8 41.0 %copy-start.3 = (f32[256,256]{1,0:T(8,128)S(1)}, f32[256,256]{1,0:T(8,128)}, u32[]{:S(2)}) copy-start(f32[256,256]{1,0:T(8,128)} %u_inv.1) | copy-start | bytes 786436
  37.8 15.5 %all-to-all-start.2 = ((f32[8,36,256]{2,1,0:T(8,128)}), f32[8,36,256]{2,1,0:T(8,128)S(1)}, u32[]{:S(2)}, u32[]{:S(2)}) async-start(f32[8,36,256]{2,1,0:T(8,128)} %plane_sum.1), calls=%async_computation.2 | async-start | bytes 655360 | tf_op jit(solution)/shard_map/all_to_all | solution.py:303
  53.4 25.5 %all-to-all-start.3 = ((f32[8,32,512]{2,1,0:T(8,128)}), f32[8,32,512]{2,1,0:T(8,128)S(1)}, u32[]{:S(2)}, u32[]{:S(2)}) async-start(f32[8,32,512]{2,1,0:T(8,128)} %panel_columns.1), calls=%async_computation.3 | async-start | bytes 1048576 | tf_op jit(solution)/shard_map/all_to_all | solution.py:305

commit v5 on v4

--- a/solution.py
+++ b/solution.py
@@ -51,13 +51,18 @@
         copy.wait()
 
 
-def pivot_kernel(place, pivots, slab, send, top_row, top_col, first, second, source_v, source_s, sem):
+def pivot_kernel(place, pivots, slab, send, top_row, top_col, first, second, source_v, source_s, sems):
     rows, columns = slab.shape
     width = pivots.shape[1]
     groups, block, _ = send.shape
     share = top_row.shape[1]
     row_start = place[0]
     share_start = place[1]
+    gives = []
+    for half, give in enumerate((first, second)):
+        start = pl.multiple_of((2 * half + place[3]) * share, share)
+        gives.append(pltpu.make_async_copy(slab.at[pl.ds(start, share)], give, sems.at[1 + half]))
+        gives[-1].start()
     along = lax.broadcasted_iota(I32, (width, width), 1)
     down = lax.broadcasted_iota(I32, (width, width), 0)
     pivot_row = pivots[...]
@@ -82,7 +87,7 @@
         lane_lookup(content, jnp.maximum(last, 0)),
     )
     source_v[...] = source
-    to_scalar = pltpu.make_async_copy(source_v, source_s, sem)
+    to_scalar = pltpu.make_async_copy(source_v, source_s, sems.at[0])
     to_scalar.start()
     content_row = content[:1]
     target_row = jnp.where((later == 0) & (pivot_row >= width), pivot_row, -1)
@@ -107,9 +112,6 @@
     owned_row = jnp.where((local_row >= 0) & (local_row < rows), 1.0, 0.0).astype(F32)
     owned_all = jnp.broadcast_to(owned_row, (width, width))
     owned = jnp.max(jnp.where(along == down, owned_all, 0.0), axis=1, keepdims=True)
-    for half, give in enumerate((first, second)):
-        start = pl.multiple_of((2 * half + place[3]) * share, share)
-        give[...] = slab[pl.ds(start, share), :]
     to_scalar.wait()
 
     def gather(group, carry):
@@ -122,6 +124,8 @@
     for group in range(groups):
         keep = owned[group * block : (group + 1) * block] > 0.0
         send[group] = jnp.where(keep, send[group], 0.0)
+    for copy in gives:
+        copy.wait()
 
 
 def pack_kernel(moved, got, send):
@@ -251,11 +255,11 @@
             jax.ShapeDtypeStruct((share, columns), F32),
         ),
         in_specs=[SMEM, VMEM, VMEM],
-        out_specs=(VMEM,) * 5,
+        out_specs=(VMEM, VMEM, VMEM, ANY, ANY),
         scratch_shapes=[
             pltpu.VMEM((8, width), I32),
             pltpu.SMEM((8, width), I32),
-            pltpu.SemaphoreType.DMA,
+            pltpu.SemaphoreType.DMA((3,)),
         ],
         compiler_params=params,
         cost_estimate=pl.CostEstimate(

time: 83.6 us -> 83.6 us (level)
  Pallas kernels: 12.8 us -> 11.9 us
    pallas_call x1, Pallas kernels: 4.4 us -> 3.48 us  [shards(): pl.pallas_call(pivot_kernel, out_shape=(jax.ShapeDtypeStruct((n_plane, bl...]
    all_to_all x1, starting transfers between devices: 7.58 us -> 8.46 us  [shards(): got = lax.all_to_all(send, PLANE, 0, 0)]
  transfers between devices with their start and end apart: 7 -> 7, of which waited for: 3 -> 4; matrix products, arithmetic and copies ran while one was open for 3% -> 3% of each run, Pallas kernels for 9% -> 8%
where the time goes in v5:
time: 83.6 us; the launch traced here: 82 us
  starting transfers between devices  39.5 us (47%)
  blocking collectives  15.3 us (18%)
  waiting for transfers between devices  13 us (16%)
  Pallas kernels  11.9 us (14%)
  other arithmetic  2.26 us (3%)
    all_gather x1, blocking collectives, shards(): rows_in = lax.all_gather(rows_out, PLANE)  15.3 us
    all_to_all x1, starting transfers between devices, shards(): panel_p = lax.all_to_all(panel_out, 'z', 0, 0)  10 us
    all_to_all x1, starting transfers between devices, shards(): got = lax.all_to_all(send, PLANE, 0, 0)  8.46 us
    all_to_all x1, starting transfers between devices, shards(): top = lax.all_to_all(top, 'y', 0, 0)  7.65 us
    all_to_all x1, waiting for transfers between devices, shards(): got = lax.all_to_all(send, 'y', 0, 0)  6.57 us
    ppermute x1, starting transfers between devices, shards(): second_got = lax.ppermute(second, 'core', swap)  4.58 us
    ppermute x1, waiting for transfers between devices, shards(): slab_got = lax.ppermute(slab_give, 'xl', swap)  3.73 us
    all_to_all x1, starting transfers between devices, shards(): got = lax.all_to_all(send, 'y', 0, 0)  3.56 us
  transfers between devices with their start and end apart: 7, of which 4 were waited for; matrix products, arithmetic and copies ran while one was open for 3% of the time, Pallas kernels for 8%

profile of v5, /device:TPU:1, one launch (start us, length us, event | category | flops | bytes accessed | tf_op | source)
XLA Modules:
  0.0 82.0 jit_solution(1811871571604501455)
XLA Ops:
  0.0 0.0 copy-start
  0.0 0.0 copy-start.4
  0.0 1.9 %top_rows.1 = f32[8,40,256]{2,1,0:T(8,128)} custom-call(f32[2048,256]{1,0:T(8,128)} %bitcast.11, f32[32,2048]{1,0:T(8,128)} %panel.3), custom_call_target="tpu_custom_call" | custom-call | tf_op jit(solution)/shard_map/top_rows/pallas_call | solution.py:236
  2.0 0.1 pad_add_fusion.place
  2.0 7.7 %all-to-all-start = ((f32[8,40,256]{2,1,0:T(8,128)}), f32[8,40,256]{2,1,0:T(8,128)S(1)}, u32[]{:S(2)}, u32[]{:S(2)}) async-start(f32[8,40,256]{2,1,0:T(8,128)} %top_rows.1), calls=%async_computation | async-start | bytes 655360 | tf_op jit(solution)/shard_map/all_to_all | solution.py:246
  9.7 0.0 copy-done
  9.7 0.0 copy-done.4
  9.7 3.5 %pivot_rows.1 = (f32[8,32,256]{2,1,0:T(8,128)S(1)}, s32[1,512]{1,0:T(1,128)S(1)}, s32[512,128]{1,0:T(8,128)S(1)}, f32[512,256]{1,0:T(8,128)}, f32[512,256]{1,0:T(8,128)}) custom-call(s32[4]{0:T(128)S(1)} %pad_add_fusion.place, s32[1,256]{1,0:T(1,128)S(1)} %bitcast.14, f32[2048,256]{1,0:T(8,128)S(1)} %bitcast.12), custom_call_target="tpu_custom_call" | custom-call | flops 268435456 | bytes 8388608 | tf_op jit(solution)/shard_map/pivot_rows/pallas_call | solution.py:248
  13.2 4.6 %collective-permute-start.1 = (f32[512,256]{1,0:T(8,128)}, f32[512,256]{1,0:T(8,128)}, u32[]{:S(2)}, u32[]{:S(2)}) collective-permute-start(f32[512,256]{1,0:T(8,128)} %get-tuple-element.17), channel_id=1, source_target_pairs={{0,1},{1,0},{2,3},{3,2},{4,5},{5,4},{6,7},{7,6},{8,9},{9,8},{10,11... | collective-permute-start | bytes 1572872 | tf_op jit(solution)/shard_map/ppermute | solution.py:280
  17.8 1.9 %collective-permute-start = (f32[512,256]{1,0:T(8,128)}, f32[512,256]{1,0:T(8,128)}, u32[]{:S(2)}, u32[]{:S(2)}) collective-permute-start(f32[512,256]{1,0:T(8,128)} %get-tuple-element.16), channel_id=1, source_target_pairs={{0,1},{1,0},{2,3},{3,2},{4,5},{5,4},{6,7},{7,6},{8,9},{9,8},{10,11... | collective-permute-start | bytes 1572872 | tf_op jit(solution)/shard_map/ppermute | solution.py:279
  19.7 0.1 all-to-all-done.got
  19.8 0.8 pack_plane.1
  20.5 8.5 %all-to-all-start.1 = ((f32[8,44,256]{2,1,0:T(8,128)}), f32[8,44,256]{2,1,0:T(8,128)S(1)}, u32[]{:S(2)}, u32[]{:S(2)}) async-start(f32[8,44,256]{2,1,0:T(8,128)} %pack_plane.1), calls=%async_computation.1 | async-start | bytes 786432 | tf_op jit(solution)/shard_map/all_to_all | solution.py:285
  29.0 0.0 copy-start.1
  29.0 0.0 collective-permute-done.1
  29.0 0.0 collective-permute-done
  29.0 2.2 %bitcast_add_fusion = (f32[512,256]{1,0:T(8,128)}, f32[512,256]{1,0:T(8,128)S(1)}) fusion(f32[512,256]{1,0:T(8,128)} %collective-permute-done.1, f32[512,256]{1,0:T(8,128)} %collective-permute-done, f32[1,2048,256]{2,1,0:T(8,128)S(1)} %copy-done, s32[]{:T(128)S(6)} %select_n.21, pred[]{:T(512)S(6)} %eq.4, s32[]{:T(128)S(6)} %select_n.18), kind=kLoop, calls=%fused_computation | loop fusion | flops 524288 | bytes 3145737 | tf_op jit(solution)/shard_map/add | solution.py:284
  31.2 3.3 %collective-permute-start.2 = (f32[512,256]{1,0:T(8,128)}, f32[512,256]{1,0:T(8,128)S(1)}, u32[]{:S(2)}, u32[]{:S(2)}) collective-permute-start(f32[512,256]{1,0:T(8,128)} %get-tuple-element.25), channel_id=1, source_target_pairs={{0,2},{2,0},{1,3},{3,1},{4,6},{6,4},{5,7},{7,5},{8,10},{10,8},{9,1... | collective-permute-start | bytes 1572872 | tf_op jit(solution)/shard_map/ppermute | solution.py:306
  34.5 2.6 %all-to-all-done.1.got = f32[8,44,256]{2,1,0:T(8,128)S(1)} async-done(((f32[8,44,256]{2,1,0:T(8,128)}), f32[8,44,256]{2,1,0:T(8,128)S(1)}, u32[]{:S(2)}, u32[]{:S(2)}) %all-to-all-start.1) | async-done | bytes 360480 | tf_op jit(solution)/shard_map/all_to_all | solution.py:285
  37.1 0.8 plane_sum.1
  37.8 0.0 copy-start.2
  37.8 3.6 %all-to-all-start.2 = ((f32[8,36,256]{2,1,0:T(8,128)}), f32[8,36,256]{2,1,0:T(8,128)S(1)}, u32[]{:S(2)}, u32[]{:S(2)}) async-start(f32[8,36,256]{2,1,0:T(8,128)} %plane_sum.1), calls=%async_computation.2 | async-start | bytes 655360 | tf_op jit(solution)/shard_map/all_to_all | solution.py:307
  41.4 0.0 copy-done.1
  41.4 1.8 %panel_columns.1 = f32[8,32,512]{2,1,0:T(8,128)} custom-call(s32[4]{0:T(128)S(1)} %pad_add_fusion.place, f32[8,44,256]{2,1,0:T(8,128)S(1)} %all-to-all-done.1.got, f32[32,2048]{1,0:T(8,128)S(1)} %copy-done.1, s32[1,512]{1,0:T(1,128)S(1)} %get-tuple-element.20.top_row), custom_call_target="tpu_custom_call" | custom-call | flops 268435456 | bytes 4194304 | tf_op jit(solution)/shard_map/panel_columns/pallas_call | solution.py:294
  43.2 3.7 %collective-permute-done.2.slab_got = f32[512,256]{1,0:T(8,128)S(1)} collective-permute-done((f32[512,256]{1,0:T(8,128)}, f32[512,256]{1,0:T(8,128)S(1)}, u32[]{:S(2)}, u32[]{:S(2)}) %collective-permute-start.2) | collective-permute-done | bytes 524320 | tf_op jit(solution)/shard_map/ppermute | solution.py:306
  46.9 6.6 %all-to-all-done.2.got = f32[8,36,256]{2,1,0:T(8,128)S(1)} async-done(((f32[8,36,256]{2,1,0:T(8,128)}), f32[8,36,256]{2,1,0:T(8,128)S(1)}, u32[]{:S(2)}, u32[]{:S(2)}) %all-to-all-start.2) | async-done | bytes 294944 | tf_op jit(solution)/shard_map/all_to_all | solution.py:307
  53.5 10.0 %all-to-all-start.3 = ((f32[8,32,512]{2,1,0:T(8,128)}), f32[8,32,512]{2,1,0:T(8,128)S(1)}, u32[]{:S(2)}, u32[]{:S(2)}) async-start(f32[8,32,512]{2,1,0:T(8,128)} %panel_columns.1), calls=%async_computation.3 | async-start | bytes 1048576 | tf_op jit(solution)/shard_map/all_to_all | solution.py:309
  63.6 15.3 %all-gather = f32[512,256]{1,0:T(8,128)S(1)} all-gather(f32[64,256]{1,0:T(8,128)S(1)} %column_sum.1), channel_id=2, replica_groups=mesh['y'=8,'xh'=2,'z'=8,'xl'=2,'core'=2] {'xh','xl','core'}, dimensions={0}, use_global_device_ids=true | all-gather | bytes 589824 | tf_op jit(solution)/shard_map/all_gather | solution.py:318
  78.8 0.0 all-to-all-done.3.panel
  78.8 0.0 copy-done.2
  78.8 0.0 copy-done.3
  78.8 3.2 %update_rows.1 = f32[512,256]{1,0:T(8,128)} custom-call(s32[4]{0:T(128)S(1)} %pad_add_fusion.place, f32[512,256]{1,0:T(8,128)S(1)} %get-tuple-element.26.slab, f32[512,256]{1,0:T(8,128)S(1)} %collective-permute-done.2.slab_got, f32[8,32,512]{2,1,0:T(8,128)S(1)} %all-to-all-done.3.panel, f32[8,64,256]{2,1,0:T(8,128)S(1)} %bitcast.13, ...), custom_call_target="tpu_custom_call" | custom-call | tf_op jit(solution)/shard_map/update_rows/pallas_call | solution.py:319
  (2 shorter events, 0.0 us)
Async XLA Ops:
  0.0 9.7 %copy-start = (f32[1,2048,256]{2,1,0:T(8,128)S(1)}, f32[1,2048,256]{2,1,0:T(8,128)}, u32[]{:S(2)}) copy-start(f32[1,2048,256]{2,1,0:T(8,128)} %param.5) | copy-start | bytes 6291460
  0.0 9.7 %copy-start.4 = (s32[256]{0:T(256)S(1)}, s32[256]{0:T(256)}, u32[]{:S(2)}) copy-start(s32[256]{0:T(256)} %param.9) | copy-start | bytes 3076
  2.0 17.7 %all-to-all-start = ((f32[8,40,256]{2,1,0:T(8,128)}), f32[8,40,256]{2,1,0:T(8,128)S(1)}, u32[]{:S(2)}, u32[]{:S(2)}) async-start(f32[8,40,256]{2,1,0:T(8,128)} %top_rows.1), calls=%async_computation | async-start | bytes 655360 | tf_op jit(solution)/shard_map/all_to_all | solution.py:246
  13.2 15.8 %collective-permute-start.1 = (f32[512,256]{1,0:T(8,128)}, f32[512,256]{1,0:T(8,128)}, u32[]{:S(2)}, u32[]{:S(2)}) collective-permute-start(f32[512,256]{1,0:T(8,128)} %get-tuple-element.17), channel_id=1, source_target_pairs={{0,1},{1,0},{2,3},{3,2},{4,5},{5,4},{6,7},{7,6},{8,9},{9,8},{10,11... | collective-permute-start | bytes 1572872 | tf_op jit(solution)/shard_map/ppermute | solution.py:280
  17.8 11.2 %collective-permute-start = (f32[512,256]{1,0:T(8,128)}, f32[512,256]{1,0:T(8,128)}, u32[]{:S(2)}, u32[]{:S(2)}) collective-permute-start(f32[512,256]{1,0:T(8,128)} %get-tuple-element.16), channel_id=1, source_target_pairs={{0,1},{1,0},{2,3},{3,2},{4,5},{5,4},{6,7},{7,6},{8,9},{9,8},{10,11... | collective-permute-start | bytes 1572872 | tf_op jit(solution)/shard_map/ppermute | solution.py:279
  20.5 16.5 %all-to-all-start.1 = ((f32[8,44,256]{2,1,0:T(8,128)}), f32[8,44,256]{2,1,0:T(8,128)S(1)}, u32[]{:S(2)}, u32[]{:S(2)}) async-start(f32[8,44,256]{2,1,0:T(8,128)} %pack_plane.1), calls=%async_computation.1 | async-start | bytes 786432 | tf_op jit(solution)/shard_map/all_to_all | solution.py:285
  29.0 12.4 %copy-start.1 = (f32[32,2048]{1,0:T(8,128)S(1)}, f32[32,2048]{1,0:T(8,128)}, u32[]{:S(2)}) copy-start(f32[32,2048]{1,0:T(8,128)} %panel.3) | copy-start | bytes 786436
  31.2 15.7 %collective-permute-start.2 = (f32[512,256]{1,0:T(8,128)}, f32[512,256]{1,0:T(8,128)S(1)}, u32[]{:S(2)}, u32[]{:S(2)}) collective-permute-start(f32[512,256]{1,0:T(8,128)} %get-tuple-element.25), channel_id=1, source_target_pairs={{0,2},{2,0},{1,3},{3,1},{4,6},{6,4},{5,7},{7,5},{8,10},{10,8},{9,1... | collective-permute-start | bytes 1572872 | tf_op jit(solution)/shard_map/ppermute | solution.py:306
  37.8 41.0 %copy-start.2 = (f32[256,256]{1,0:T(8,128)S(1)}, f32[256,256]{1,0:T(8,128)}, u32[]{:S(2)}) copy-start(f32[256,256]{1,0:T(8,128)} %l_inv.1) | copy-start | bytes 786436
  37.8 41.0 %copy-start.3 = (f32[256,256]{1,0:T(8,128)S(1)}, f32[256,256]{1,0:T(8,128)}, u32[]{:S(2)}) copy-start(f32[256,256]{1,0:T(8,128)} %u_inv.1) | copy-start | bytes 786436
  37.8 15.7 %all-to-all-start.2 = ((f32[8,36,256]{2,1,0:T(8,128)}), f32[8,36,256]{2,1,0:T(8,128)S(1)}, u32[]{:S(2)}, u32[]{:S(2)}) async-start(f32[8,36,256]{2,1,0:T(8,128)} %plane_sum.1), calls=%async_computation.2 | async-start | bytes 655360 | tf_op jit(solution)/shard_map/all_to_all | solution.py:307
  53.5 25.3 %all-to-all-start.3 = ((f32[8,32,512]{2,1,0:T(8,128)}), f32[8,32,512]{2,1,0:T(8,128)S(1)}, u32[]{:S(2)}, u32[]{:S(2)}) async-start(f32[8,32,512]{2,1,0:T(8,128)} %panel_columns.1), calls=%async_computation.3 | async-start | bytes 1048576 | tf_op jit(solution)/shard_map/all_to_all | solution.py:309

commit v6 on v5

--- a/solution.py
+++ b/solution.py
@@ -33,21 +33,27 @@
     return jnp.concatenate(parts, axis=1)
 
 
-def top_kernel(slab, panel, send, sems, *, layers):
+def top_kernel(slab, panel, send, staged, sems, *, layers):
     groups, both, _ = send.shape
     fill = panel.shape[0] // layers
     block = both - fill
     width = groups * block
     start = pl.multiple_of(lax.axis_index(DEPTH) * fill, fill)
-    copies = []
+    arrivals, departures = [], []
     for target in range(groups):
         rows = slab.at[pl.ds(target * block, block), :]
         part = panel.at[pl.ds(start, fill), pl.ds(0, width)]
-        copies.append(pltpu.make_async_copy(rows, send.at[target, pl.ds(0, block)], sems.at[0, target]))
-        copies.append(pltpu.make_async_copy(part, send.at[target, pl.ds(block, fill)], sems.at[1, target]))
-    for copy in copies:
+        here = staged.at[target]
+        arrivals.append(pltpu.make_async_copy(rows, here.at[pl.ds(0, block)], sems.at[0, target]))
+        arrivals.append(pltpu.make_async_copy(part, here.at[pl.ds(block, fill)], sems.at[1, target]))
+        departures.append(pltpu.make_async_copy(here, send.at[target], sems.at[2, target]))
+    for copy in arrivals:
         copy.start()
-    for copy in copies:
+    for target in range(groups):
+        arrivals[2 * target].wait()
+        arrivals[2 * target + 1].wait()
+        departures[target].start()
+    for copy in departures:
         copy.wait()
 
 
@@ -237,8 +243,11 @@
         functools.partial(top_kernel, layers=n_depth),
         out_shape=jax.ShapeDtypeStruct((n_y, width // n_y + fill, columns), F32),
         in_specs=[ANY, ANY],
-        out_specs=VMEM,
-        scratch_shapes=[pltpu.SemaphoreType.DMA((2, n_y))],
+        out_specs=ANY,
+        scratch_shapes=[
+            pltpu.VMEM((n_y, width // n_y + fill, columns), F32),
+            pltpu.SemaphoreType.DMA((3, n_y)),
+        ],
         compiler_params=wide,
         name="top_rows",
     )(slab_local, panel_t)

time: 83.6 us -> 83.6 us (level)
  transfers between devices with their start and end apart: 7 -> 7, of which waited for: 4 -> 3; matrix products, arithmetic and copies ran while one was open for 3% -> 3% of each run, Pallas kernels for 8% -> 8%
where the time goes in v6:
time: 83.6 us; the launch traced here: 82.1 us
  starting transfers between devices  39.5 us (47%)
  blocking collectives  15.3 us (18%)
  waiting for transfers between devices  13 us (16%)
  Pallas kernels  12 us (14%)
  other arithmetic  2.26 us (3%)
    all_gather x1, blocking collectives, shards(): rows_in = lax.all_gather(rows_out, PLANE)  15.3 us
    all_to_all x1, starting transfers between devices, shards(): panel_p = lax.all_to_all(panel_out, 'z', 0, 0)  10 us
    all_to_all x1, starting transfers between devices, shards(): got = lax.all_to_all(send, PLANE, 0, 0)  8.47 us
    all_to_all x1, starting transfers between devices, shards(): top = lax.all_to_all(top, 'y', 0, 0)  7.65 us
    all_to_all x1, waiting for transfers between devices, shards(): got = lax.all_to_all(send, 'y', 0, 0)  6.57 us
    ppermute x1, starting transfers between devices, shards(): second_got = lax.ppermute(second, 'core', swap)  4.58 us
    ppermute x1, waiting for transfers between devices, shards(): slab_got = lax.ppermute(slab_give, 'xl', swap)  3.73 us
    all_to_all x1, starting transfers between devices, shards(): got = lax.all_to_all(send, 'y', 0, 0)  3.56 us
  transfers between devices with their start and end apart: 7, of which 3 were waited for; matrix products, arithmetic and copies ran while one was open for 3% of the time, Pallas kernels for 8%

profile of v6, /device:TPU:1, one launch (start us, length us, event | category | flops | bytes accessed | tf_op | source)
XLA Modules:
  0.0 82.1 jit_solution(11486044124168430187)
XLA Ops:
  0.0 0.0 copy-start
  0.0 0.0 copy-start.4
  0.0 2.0 %top_rows.1 = f32[8,40,256]{2,1,0:T(8,128)} custom-call(f32[2048,256]{1,0:T(8,128)} %bitcast.11, f32[32,2048]{1,0:T(8,128)} %panel.3), custom_call_target="tpu_custom_call" | custom-call | tf_op jit(solution)/shard_map/top_rows/pallas_call | solution.py:242
  2.0 0.1 pad_add_fusion.place
  2.1 7.7 %all-to-all-start = ((f32[8,40,256]{2,1,0:T(8,128)}), f32[8,40,256]{2,1,0:T(8,128)S(1)}, u32[]{:S(2)}, u32[]{:S(2)}) async-start(f32[8,40,256]{2,1,0:T(8,128)} %top_rows.1), calls=%async_computation | async-start | bytes 655360 | tf_op jit(solution)/shard_map/all_to_all | solution.py:255
  9.7 0.0 copy-done
  9.7 0.0 copy-done.4
  9.7 3.5 %pivot_rows.1 = (f32[8,32,256]{2,1,0:T(8,128)S(1)}, s32[1,512]{1,0:T(1,128)S(1)}, s32[512,128]{1,0:T(8,128)S(1)}, f32[512,256]{1,0:T(8,128)}, f32[512,256]{1,0:T(8,128)}) custom-call(s32[4]{0:T(128)S(1)} %pad_add_fusion.place, s32[1,256]{1,0:T(1,128)S(1)} %bitcast.14, f32[2048,256]{1,0:T(8,128)S(1)} %bitcast.12), custom_call_target="tpu_custom_call" | custom-call | flops 268435456 | bytes 8388608 | tf_op jit(solution)/shard_map/pivot_rows/pallas_call | solution.py:257
  13.2 4.6 %collective-permute-start.1 = (f32[512,256]{1,0:T(8,128)}, f32[512,256]{1,0:T(8,128)}, u32[]{:S(2)}, u32[]{:S(2)}) collective-permute-start(f32[512,256]{1,0:T(8,128)} %get-tuple-element.17), channel_id=1, source_target_pairs={{0,1},{1,0},{2,3},{3,2},{4,5},{5,4},{6,7},{7,6},{8,9},{9,8},{10,11... | collective-permute-start | bytes 1572872 | tf_op jit(solution)/shard_map/ppermute | solution.py:289
  17.8 1.9 %collective-permute-start = (f32[512,256]{1,0:T(8,128)}, f32[512,256]{1,0:T(8,128)}, u32[]{:S(2)}, u32[]{:S(2)}) collective-permute-start(f32[512,256]{1,0:T(8,128)} %get-tuple-element.16), channel_id=1, source_target_pairs={{0,1},{1,0},{2,3},{3,2},{4,5},{5,4},{6,7},{7,6},{8,9},{9,8},{10,11... | collective-permute-start | bytes 1572872 | tf_op jit(solution)/shard_map/ppermute | solution.py:288
  19.7 0.0 all-to-all-done.got
  19.8 0.8 pack_plane.1
  20.6 8.5 %all-to-all-start.1 = ((f32[8,44,256]{2,1,0:T(8,128)}), f32[8,44,256]{2,1,0:T(8,128)S(1)}, u32[]{:S(2)}, u32[]{:S(2)}) async-start(f32[8,44,256]{2,1,0:T(8,128)} %pack_plane.1), calls=%async_computation.1 | async-start | bytes 786432 | tf_op jit(solution)/shard_map/all_to_all | solution.py:294
  29.0 0.0 copy-start.1
  29.0 0.0 collective-permute-done.1
  29.0 0.0 collective-permute-done
  29.0 2.2 %bitcast_add_fusion = (f32[512,256]{1,0:T(8,128)}, f32[512,256]{1,0:T(8,128)S(1)}) fusion(f32[512,256]{1,0:T(8,128)} %collective-permute-done.1, f32[512,256]{1,0:T(8,128)} %collective-permute-done, f32[1,2048,256]{2,1,0:T(8,128)S(1)} %copy-done, s32[]{:T(128)S(6)} %select_n.21, pred[]{:T(512)S(6)} %eq.4, s32[]{:T(128)S(6)} %select_n.18), kind=kLoop, calls=%fused_computation | loop fusion | flops 524288 | bytes 3145737 | tf_op jit(solution)/shard_map/add | solution.py:293
  31.2 3.3 %collective-permute-start.2 = (f32[512,256]{1,0:T(8,128)}, f32[512,256]{1,0:T(8,128)S(1)}, u32[]{:S(2)}, u32[]{:S(2)}) collective-permute-start(f32[512,256]{1,0:T(8,128)} %get-tuple-element.25), channel_id=1, source_target_pairs={{0,2},{2,0},{1,3},{3,1},{4,6},{6,4},{5,7},{7,5},{8,10},{10,8},{9,1... | collective-permute-start | bytes 1572872 | tf_op jit(solution)/shard_map/ppermute | solution.py:315
  34.5 2.6 %all-to-all-done.1.got = f32[8,44,256]{2,1,0:T(8,128)S(1)} async-done(((f32[8,44,256]{2,1,0:T(8,128)}), f32[8,44,256]{2,1,0:T(8,128)S(1)}, u32[]{:S(2)}, u32[]{:S(2)}) %all-to-all-start.1) | async-done | bytes 360480 | tf_op jit(solution)/shard_map/all_to_all | solution.py:294
  37.1 0.8 plane_sum.1
  37.9 0.0 copy-start.2
  37.9 3.6 %all-to-all-start.2 = ((f32[8,36,256]{2,1,0:T(8,128)}), f32[8,36,256]{2,1,0:T(8,128)S(1)}, u32[]{:S(2)}, u32[]{:S(2)}) async-start(f32[8,36,256]{2,1,0:T(8,128)} %plane_sum.1), calls=%async_computation.2 | async-start | bytes 655360 | tf_op jit(solution)/shard_map/all_to_all | solution.py:316
  41.4 0.0 copy-done.1
  41.4 1.8 %panel_columns.1 = f32[8,32,512]{2,1,0:T(8,128)} custom-call(s32[4]{0:T(128)S(1)} %pad_add_fusion.place, f32[8,44,256]{2,1,0:T(8,128)S(1)} %all-to-all-done.1.got, f32[32,2048]{1,0:T(8,128)S(1)} %copy-done.1, s32[1,512]{1,0:T(1,128)S(1)} %get-tuple-element.20.top_row), custom_call_target="tpu_custom_call" | custom-call | flops 268435456 | bytes 4194304 | tf_op jit(solution)/shard_map/panel_columns/pallas_call | solution.py:303
  43.2 3.7 %collective-permute-done.2.slab_got = f32[512,256]{1,0:T(8,128)S(1)} collective-permute-done((f32[512,256]{1,0:T(8,128)}, f32[512,256]{1,0:T(8,128)S(1)}, u32[]{:S(2)}, u32[]{:S(2)}) %collective-permute-start.2) | collective-permute-done | bytes 524320 | tf_op jit(solution)/shard_map/ppermute | solution.py:315
  47.0 6.6 %all-to-all-done.2.got = f32[8,36,256]{2,1,0:T(8,128)S(1)} async-done(((f32[8,36,256]{2,1,0:T(8,128)}), f32[8,36,256]{2,1,0:T(8,128)S(1)}, u32[]{:S(2)}, u32[]{:S(2)}) %all-to-all-start.2) | async-done | bytes 294944 | tf_op jit(solution)/shard_map/all_to_all | solution.py:316
  53.5 10.0 %all-to-all-start.3 = ((f32[8,32,512]{2,1,0:T(8,128)}), f32[8,32,512]{2,1,0:T(8,128)S(1)}, u32[]{:S(2)}, u32[]{:S(2)}) async-start(f32[8,32,512]{2,1,0:T(8,128)} %panel_columns.1), calls=%async_computation.3 | async-start | bytes 1048576 | tf_op jit(solution)/shard_map/all_to_all | solution.py:318
  63.6 15.3 %all-gather = f32[512,256]{1,0:T(8,128)S(1)} all-gather(f32[64,256]{1,0:T(8,128)S(1)} %column_sum.1), channel_id=2, replica_groups=mesh['y'=8,'xh'=2,'z'=8,'xl'=2,'core'=2] {'xh','xl','core'}, dimensions={0}, use_global_device_ids=true | all-gather | bytes 589824 | tf_op jit(solution)/shard_map/all_gather | solution.py:327
  78.9 0.0 all-to-all-done.3.panel
  78.9 0.0 copy-done.2
  78.9 0.0 copy-done.3
  78.9 3.2 %update_rows.1 = f32[512,256]{1,0:T(8,128)} custom-call(s32[4]{0:T(128)S(1)} %pad_add_fusion.place, f32[512,256]{1,0:T(8,128)S(1)} %get-tuple-element.26.slab, f32[512,256]{1,0:T(8,128)S(1)} %collective-permute-done.2.slab_got, f32[8,32,512]{2,1,0:T(8,128)S(1)} %all-to-all-done.3.panel, f32[8,64,256]{2,1,0:T(8,128)S(1)} %bitcast.13, ...), custom_call_target="tpu_custom_call" | custom-call | tf_op jit(solution)/shard_map/update_rows/pallas_call | solution.py:328
  (2 shorter events, 0.0 us)
Async XLA Ops:
  0.0 9.7 %copy-start = (f32[1,2048,256]{2,1,0:T(8,128)S(1)}, f32[1,2048,256]{2,1,0:T(8,128)}, u32[]{:S(2)}) copy-start(f32[1,2048,256]{2,1,0:T(8,128)} %param.5) | copy-start | bytes 6291460
  0.0 9.7 %copy-start.4 = (s32[256]{0:T(256)S(1)}, s32[256]{0:T(256)}, u32[]{:S(2)}) copy-start(s32[256]{0:T(256)} %param.9) | copy-start | bytes 3076
  2.1 17.7 %all-to-all-start = ((f32[8,40,256]{2,1,0:T(8,128)}), f32[8,40,256]{2,1,0:T(8,128)S(1)}, u32[]{:S(2)}, u32[]{:S(2)}) async-start(f32[8,40,256]{2,1,0:T(8,128)} %top_rows.1), calls=%async_computation | async-start | bytes 655360 | tf_op jit(solution)/shard_map/all_to_all | solution.py:255
  13.2 15.8 %collective-permute-start.1 = (f32[512,256]{1,0:T(8,128)}, f32[512,256]{1,0:T(8,128)}, u32[]{:S(2)}, u32[]{:S(2)}) collective-permute-start(f32[512,256]{1,0:T(8,128)} %get-tuple-element.17), channel_id=1, source_target_pairs={{0,1},{1,0},{2,3},{3,2},{4,5},{5,4},{6,7},{7,6},{8,9},{9,8},{10,11... | collective-permute-start | bytes 1572872 | tf_op jit(solution)/shard_map/ppermute | solution.py:289
  17.8 11.2 %collective-permute-start = (f32[512,256]{1,0:T(8,128)}, f32[512,256]{1,0:T(8,128)}, u32[]{:S(2)}, u32[]{:S(2)}) collective-permute-start(f32[512,256]{1,0:T(8,128)} %get-tuple-element.16), channel_id=1, source_target_pairs={{0,1},{1,0},{2,3},{3,2},{4,5},{5,4},{6,7},{7,6},{8,9},{9,8},{10,11... | collective-permute-start | bytes 1572872 | tf_op jit(solution)/shard_map/ppermute | solution.py:288
  20.6 16.5 %all-to-all-start.1 = ((f32[8,44,256]{2,1,0:T(8,128)}), f32[8,44,256]{2,1,0:T(8,128)S(1)}, u32[]{:S(2)}, u32[]{:S(2)}) async-start(f32[8,44,256]{2,1,0:T(8,128)} %pack_plane.1), calls=%async_computation.1 | async-start | bytes 786432 | tf_op jit(solution)/shard_map/all_to_all | solution.py:294
  29.0 12.4 %copy-start.1 = (f32[32,2048]{1,0:T(8,128)S(1)}, f32[32,2048]{1,0:T(8,128)}, u32[]{:S(2)}) copy-start(f32[32,2048]{1,0:T(8,128)} %panel.3) | copy-start | bytes 786436
  31.2 15.7 %collective-permute-start.2 = (f32[512,256]{1,0:T(8,128)}, f32[512,256]{1,0:T(8,128)S(1)}, u32[]{:S(2)}, u32[]{:S(2)}) collective-permute-start(f32[512,256]{1,0:T(8,128)} %get-tuple-element.25), channel_id=1, source_target_pairs={{0,2},{2,0},{1,3},{3,1},{4,6},{6,4},{5,7},{7,5},{8,10},{10,8},{9,1... | collective-permute-start | bytes 1572872 | tf_op jit(solution)/shard_map/ppermute | solution.py:315
  37.9 41.0 %copy-start.2 = (f32[256,256]{1,0:T(8,128)S(1)}, f32[256,256]{1,0:T(8,128)}, u32[]{:S(2)}) copy-start(f32[256,256]{1,0:T(8,128)} %l_inv.1) | copy-start | bytes 786436
  37.9 41.0 %copy-start.3 = (f32[256,256]{1,0:T(8,128)S(1)}, f32[256,256]{1,0:T(8,128)}, u32[]{:S(2)}) copy-start(f32[256,256]{1,0:T(8,128)} %u_inv.1) | copy-start | bytes 786436
  37.9 15.7 %all-to-all-start.2 = ((f32[8,36,256]{2,1,0:T(8,128)}), f32[8,36,256]{2,1,0:T(8,128)S(1)}, u32[]{:S(2)}, u32[]{:S(2)}) async-start(f32[8,36,256]{2,1,0:T(8,128)} %plane_sum.1), calls=%async_computation.2 | async-start | bytes 655360 | tf_op jit(solution)/shard_map/all_to_all | solution.py:316
  53.5 25.3 %all-to-all-start.3 = ((f32[8,32,512]{2,1,0:T(8,128)}), f32[8,32,512]{2,1,0:T(8,128)S(1)}, u32[]{:S(2)}, u32[]{:S(2)}) async-start(f32[8,32,512]{2,1,0:T(8,128)} %panel_columns.1), calls=%async_computation.3 | async-start | bytes 1048576 | tf_op jit(solution)/shard_map/all_to_all | solution.py:318
